TPU v7x, 32 devices: a whole 2x2x4 slice. The times are simulated.
32 devices in a mesh: ctx: 8 (over z, y), tp: 4 (over x, core).
Axes of the slice: x: 2, y: 2, z: 4, core: 2. Of those that a mesh axis runs over, the one named last changes fastest.
Arguments:
- features: bfloat16 [1024, 3, 4096], P('ctx', None, 'tp'), may hold values from -6 to 6
- short_taps: float32 [3, 3, 4096], P(None, None, 'tp'), may hold values from -3 to 3
- residues: float32 [16, 4096], P(None, 'tp'), may hold values from -2 to 2
- log_rate: float32 [16, 4096], P(None, 'tp'), may hold values from -13 to -3.5, as said below
- out_weight: bfloat16 [4096, 8192], P('tp'), may hold values from -0.09375 to 0.09375
- grad_out: bfloat16 [1024, 8192], P('ctx', 'tp'), may hold values from -6 to 6
Outputs:
- grad_features: bfloat16 [1024, 3, 4096], P('ctx', None, 'tp')
- grad_taps: float32 [3, 3, 4096], P(None, None, 'tp')
- grad_residues: float32 [16, 4096], P(None, 'tp')
- grad_log_rate: float32 [16, 4096], P(None, 'tp')
- grad_weight_t: float32 [8192, 4096], P('ctx', 'tp')
Inputs may be any that keep to these rules, and one draw needn't show every extreme that they name: `log_rate`: log of a decay rate per token.
All inputs are finite; a program needn't handle non-finite values.
Results may differ from a plain program's by a relative error of at most 0.0058.
Values may be sent and summed in bfloat16 or wider, within the bound.
A program may use at most 192 MiB of HBM per device.

v0:
```python
import jax
import jax.numpy as jnp
from jax import lax
from jax.sharding import PartitionSpec as P


def shifted(value, axis, steps):
    count = lax.axis_size(axis)
    first, last = (max(0, -steps), min(count, count - steps))
    return lax.ppermute(value, axis, [(source, source + steps) for source in range(first, last)])


def block_tables(residues, log_rate, block_len):
    decay_rate = jnp.exp(log_rate)
    amplitude = residues * jnp.exp(0.5 * log_rate)
    lag_steps = jnp.arange(block_len).astype(jnp.float32)
    kernel = jnp.sum(
        amplitude[:, None, :] * jnp.exp(-decay_rate[:, None, :] * lag_steps[None, :, None]), axis=0
    )
    row_ids = jnp.arange(block_len)[:, None]
    col_ids = jnp.arange(block_len)[None, :]
    distance = row_ids - col_ids
    toeplitz = jnp.where((distance >= 0)[:, :, None], kernel[jnp.maximum(distance, 0)], 0.0)
    injection = jnp.exp(-decay_rate[:, None, :] * (block_len - 1 - lag_steps)[None, :, None])
    readout = amplitude[:, None, :] * jnp.exp(
        -decay_rate[:, None, :] * (lag_steps + 1.0)[None, :, None]
    )
    return (decay_rate, toeplitz, injection, readout)


def combine_states(earlier, later):
    return (earlier[0] * later[0], later[0] * earlier[1] + later[1])


def long_conv(product, residues, log_rate):
    block_len = 128
    length, channels = product.shape
    block_count = length // block_len
    decay_rate, toeplitz, injection, readout = block_tables(residues, log_rate, block_len)
    blocks = product.reshape(block_count, block_len, channels)
    inside = jnp.einsum("ijc,bjc->bic", toeplitz, blocks, precision=lax.Precision.HIGHEST)
    entering = jnp.einsum("rjc,bjc->brc", injection, blocks, precision=lax.Precision.HIGHEST)
    carry_decay = jnp.broadcast_to(jnp.exp(-decay_rate * block_len), entering.shape)
    unused, states = lax.associative_scan(combine_states, (carry_decay, entering), axis=0)
    before = jnp.concatenate([jnp.zeros_like(states[:1]), states[:-1]], axis=0)
    from_past = jnp.einsum("ric,brc->bic", readout, before, precision=lax.Precision.HIGHEST)
    return (inside + from_past).reshape(length, channels)


def to_channels(values):
    return lax.all_to_all(values, "ctx", split_axis=1, concat_axis=0, tiled=True)


def to_tokens(values):
    return lax.all_to_all(values, "ctx", split_axis=0, concat_axis=1, tiled=True)


def per_device(features, short_taps, residues, log_rate, out_weight, grad_out):
    length = features.shape[0]
    tap_count = short_taps.shape[0]
    groups = lax.axis_size("ctx")
    position = lax.axis_index("ctx")
    rim_rows = shifted(features[length - (tap_count - 1) :], "ctx", 1)
    padded_in = jnp.concatenate([rim_rows, features], axis=0).astype(jnp.float32)
    shortened = sum(
        (
            short_taps[lag] * padded_in[tap_count - 1 - lag : tap_count - 1 - lag + length]
            for lag in range(tap_count)
        )
    )
    product = (shortened[:, 1] * shortened[:, 2]).astype(jnp.bfloat16)
    chan_width = product.shape[1] // groups
    local_residues = lax.dynamic_slice_in_dim(residues, position * chan_width, chan_width, 1)
    local_rates = lax.dynamic_slice_in_dim(log_rate, position * chan_width, chan_width, 1)
    product_chan = to_channels(product).astype(jnp.float32)
    conv_chan, pullback = jax.vjp(long_conv, product_chan, local_residues, local_rates)
    convolved = to_tokens(conv_chan.astype(jnp.bfloat16)).astype(jnp.float32)
    gated = (shortened[:, 0] * convolved).astype(jnp.bfloat16)
    cotangent = lax.all_gather(grad_out, "tp", axis=1, tiled=True)
    grad_weight_t = lax.psum_scatter(
        lax.dot_general(
            cotangent, gated, (((0,), (0,)), ((), ())), preferred_element_type=jnp.float32
        ),
        "ctx",
        scatter_dimension=0,
        tiled=True,
    )
    grad_gated = lax.dot_general(
        cotangent, out_weight, (((1,), (1,)), ((), ())), preferred_element_type=jnp.float32
    )
    grad_conv = (grad_gated * shortened[:, 0]).astype(jnp.bfloat16)
    grad_prod_chan, grad_res_local, grad_rate_local = pullback(
        to_channels(grad_conv).astype(jnp.float32)
    )
    grad_product = to_tokens(grad_prod_chan.astype(jnp.bfloat16)).astype(jnp.float32)
    grad_residues, grad_log_rate = (
        lax.all_gather(grad_res_local, "ctx", axis=1, tiled=True),
        lax.all_gather(grad_rate_local, "ctx", axis=1, tiled=True),
    )
    grad_short = jnp.stack(
        [grad_gated * convolved, grad_product * shortened[:, 2], grad_product * shortened[:, 1]],
        axis=1,
    )
    tail_rows = shifted(grad_short[: tap_count - 1], "ctx", -1)
    tail_pad = jnp.concatenate([grad_short, tail_rows], axis=0)
    grad_features = sum(
        (short_taps[lag] * tail_pad[lag : lag + length] for lag in range(tap_count))
    )
    partial_taps = jnp.stack(
        [
            jnp.sum(
                grad_short * padded_in[tap_count - 1 - lag : tap_count - 1 - lag + length], axis=0
            )
            for lag in range(tap_count)
        ],
        axis=0,
    )
    grad_taps = lax.psum(partial_taps, "ctx")
    return (
        grad_features.astype(jnp.bfloat16),
        grad_taps,
        grad_residues,
        grad_log_rate,
        grad_weight_t,
    )


def solution(mesh):
    return jax.shard_map(
        per_device,
        mesh=mesh,
        in_specs=(
            P("ctx", None, "tp"),
            P(None, None, "tp"),
            P(None, "tp"),
            P(None, "tp"),
            P("tp", None),
            P("ctx", "tp"),
        ),
        out_specs=(
            P("ctx", None, "tp"),
            P(None, None, "tp"),
            P(None, "tp"),
            P(None, "tp"),
            P("ctx", "tp"),
        ),
        check_vma=False,
    )
```

profile of v0, /device:TPU:13, one launch (start us, length us, event | category | flops | bytes accessed | tf_op | source)
XLA Modules:
  0.0 875.6 jit_solution(6375209423134570061)
XLA Ops:
  8.7 3.1 collective-permute-start
  14.6 1.4 maximum_convert_fusion
  17.2 1.8 copy.151
  19.0 4.7 all-to-all-start
  25.7 3.8 all-to-all-done
  29.5 2.8 fusion.16
  32.3 1.2 copy.128
  33.7 12.9 %multiply_convert_fusion.1 = (bf16[128,1024]{1,0:T(8,128)(2,1)}, f32[128,1024]{1,0:T(8,128)}) fusion(f32[128,3,1024]{2,0,1:T(8,128)S(1)} %multiply_add_fusion, bf16[128,8192]{1,0:T(8,128)(2,1)} %all-gather.2.cloned.1.call-done, bf16[1024,8192]{1,0:T(8,128)(2,1)} %param.10), kind=kOutput, calls=%fused_computation.43 | convolution fusion | flops 2147745792 | bytes 20185088 | tf_op jit(solution)/shard_map/dot_general | solution.py:88
  46.6 1.8 copy.153
  48.4 6.3 all-to-all-start.2
  57.9 3.2 pad.240
  61.1 3.0 fusion.11
  64.1 1.8 copy.134
  67.4 1.3 pad_maximum_fusion.3
  68.8 1.8 pad.157
  71.4 1.0 copy.156
  72.4 3.3 fusion.13
  75.7 5.6 select_bitcast_fusion
  81.3 9.3 %copy.155 = f32[128,128,128]{2,1,0:T(8,128)} copy(f32[128,128,128]{1,0,2:T(8,128)} %select_bitcast_fusion) | data formatting | bytes 16777216 | tf_op jit(solution)/shard_map/transpose(jvp(jit(_where)))/select_n | solution.py:23
  90.6 98.5 %scatter_custom_fusion = f32[128,128]{1,0:T(8,128)S(1)} fusion(s32[16384]{0:T(1024)} %maximum_bitcast_fusion, f32[16384,128]{1,0:T(8,128)} %bitcast.83, f32[]{:T(128)} %constant.7.clone.1), kind=kCustom, calls=%fused_computation.85 | custom fusion | flops 2097152 | bytes 66048 | tf_op jit(solution)/shard_map/transpose(jvp())/scatter-add | solution.py:23
  189.9 4.6 multiply_reduce_fusion.4
  194.5 0.9 copy.124
  195.4 54.8 %gather_fusion = f32[16384,128]{1,0:T(8,128)} fusion(f32[128,128]{1,0:T(8,128)S(1)} %copy.124, s32[16384]{0:T(1024)S(1)} %broadcast_clamp_fusion), kind=kCustom, calls=%fused_computation | custom fusion | bytes 16842752 | tf_op jit(solution)/shard_map/jvp()/gather | solution.py:23
  250.2 9.9 %broadcast_select_fusion = f32[128,128,128]{2,1,0:T(8,128)} fusion(f32[128,128,128]{2,1,0:T(8,128)} %bitcast.82, pred[128,128]{1,0:T(8,128)(4,1)} %subtract_compare_fusion), kind=kLoop, calls=%fused_computation.4 | loop fusion | flops 2097152 | bytes 16793600 | tf_op jit(solution)/shard_map/jvp(jit(_where))/select_n | solution.py:23
  260.1 9.3 %copy.126 = f32[128,128,128]{1,0,2:T(8,128)} copy(f32[128,128,128]{2,1,0:T(8,128)} %broadcast_select_fusion) | data formatting | bytes 16777216 | tf_op jit(solution)/shard_map/jvp(jit(_where))/select_n | solution.py:23
  269.4 10.1 %fusion.9 = bf16[8,128,128]{1,0,2:T(8,128)(2,1)S(1)} fusion(f32[128,8,128]{2,1,0:T(8,128)} %fusion.13, f32[128,128,128]{1,0,2:T(8,128)} %copy.126, bf16[128,8,128]{0,2,1:T(8,128)(2,1)} %all-to-all-done), kind=kOutput, calls=%fused_computation.26 | convolution fusion | flops 201588736 | bytes 9437184 | tf_op jit(solution)/shard_map/jvp(ijc,bjc->bic)/dot_general | solution.py:41
  279.5 11.1 %all_to_all.43 = bf16[8,128,128]{1,2,0:T(8,128)(2,1)S(1)} all-to-all(bf16[8,128,128]{1,2,0:T(8,128)(2,1)S(1)} %copy.130), channel_id=1, replica_groups=mesh['ctx'=8,'tp'=4] {'ctx'}, dimensions={0} | all-to-all | bytes 524288 | tf_op jit(solution)/shard_map/all_to_all | solution.py:55
  291.5 2.0 copy.152
  293.5 17.4 %convolution_bitcast_fusion = f32[8192,1024]{0,1:T(8,128)} fusion(bf16[128,8192]{1,0:T(8,128)(2,1)} %all-gather.2.cloned.1.call-done, f32[128,1024]{1,0:T(8,128)} %copy.152, f32[128,3,1024]{2,0,1:T(8,128)S(1)} %multiply_add_fusion), kind=kOutput, calls=%fused_computation.2 | convolution fusion | flops 2147745792 | bytes 36700160 | tf_op jit(solution)/shard_map/dot_general | solution.py:81
  311.0 1.3 split.21
  314.4 1.9 pad.134
  316.3 1.4 multiply_add_fusion.1
  317.8 2.6 pad.113
  321.3 1.0 copy.135
  322.3 2.2 fusion.15
  324.6 7.5 fusion.8
  332.8 5.5 all-to-all-start.3
  338.3 3.3 fusion.5
  347.1 24.0 %all_gather.11 = f32[16,1024]{1,0:T(8,128)S(1)} all-gather(f32[16,128]{1,0:T(8,128)S(1)} %get-tuple-element.56), channel_id=1, replica_groups=mesh['ctx'=8,'tp'=4] {'ctx'}, dimensions={1}, use_global_device_ids=true | all-gather | bytes 73728 | tf_op jit(solution)/shard_map/all_gather | solution.py:98
  371.1 1.8 convert_element_type.104
  372.9 2.0 copy.154
  375.0 1.3 multiply_bitcast_fusion
  376.5 1.9 collective-permute-start.1
  378.5 25.1 %all_gather.10 = f32[16,1024]{1,0:T(8,128)S(1)} all-gather(f32[16,128]{1,0:T(8,128)S(1)} %get-tuple-element.57), channel_id=1, replica_groups=mesh['ctx'=8,'tp'=4] {'ctx'}, dimensions={1}, use_global_device_ids=true | all-gather | bytes 73728 | tf_op jit(solution)/shard_map/all_gather | solution.py:97
  403.8 1.9 multiply_reduce_fusion.2
  405.7 30.0 %psum.7 = f32[3,3,1024]{2,1,0:T(4,128)} all-reduce(f32[3,3,1024]{2,1,0:T(4,128)S(1)} %pad_maximum_fusion.2), channel_id=1, replica_groups=mesh['ctx'=8,'tp'=4] {'ctx'}, use_global_device_ids=true, to_apply=%region_4.5 | all-reduce | flops 9216 | bytes 73728 | tf_op jit(solution)/shard_map/psum | solution.py:118
  435.7 426.2 %reduce-scatter.2.cloned.1.call-done = f32[1024,1024]{0,1:T(8,128)} async-done(((f32[8192,1024]{0,1:T(8,128)}), f32[1024,1024]{0,1:T(8,128)}) %reduce-scatter.2.cloned.1.call-update) | async-done | bytes 4194320 | tf_op jit(solution)/shard_map/reduce_scatter | solution.py:80
  861.9 5.3 copy.150
  (119 shorter events, 25.5 us)
Async XLA Ops:
  7.2 26.5 %all-gather.2.cloned.1.call-start = ((), (), s32[]{:S(2)}) async-start(), calls=%async_computation.5 | async-start | bytes 2621440 | tf_op jit(solution)/shard_map/all_gather | solution.py:79
  8.7 5.8 collective-permute-start
  11.9 17.6 %copy-start.20 = (f32[128]{0:T(128)}, f32[128]{0:T(128)S(1)}, u32[]{:S(2)}) copy-start(f32[128]{0:T(128)S(1)} %broadcast_subtract_fusion) | copy-start | bytes 1540
  13.2 20.3 %copy-start.15 = (f32[16,128]{1,0:T(8,128)}, f32[16,128]{1,0:T(8,128)S(1)}, u32[]{:S(2)}) copy-start(f32[16,128]{1,0:T(8,128)S(1)} %get-tuple-element.51) | copy-start | bytes 24580
  14.0 2.4 copy-start.3
  14.0 2.4 copy-start.5
  14.1 2.4 copy-start.7
  19.0 10.5 %all-to-all-start = ((bf16[128,8,128]{0,2,1:T(8,128)(2,1)}), bf16[128,8,128]{0,2,1:T(8,128)(2,1)}, u32[]{:S(2)}, u32[]{:S(2)}) async-start(bf16[128,8,128]{0,2,1:T(8,128)(2,1)} %bitcast.87), calls=%async_computation | async-start | bytes 524288 | tf_op jit(solution)/shard_map/all_to_all | solution.py:51
  33.6 21.7 %copy-start.17 = (f32[2,16,128]{2,1,0:T(8,128)}, f32[2,16,128]{2,1,0:T(8,128)S(1)}, u32[]{:S(2)}) copy-start(f32[2,16,128]{2,1,0:T(8,128)S(1)} %slice_add_fusion.3) | copy-start | bytes 49156
  48.4 12.6 %all-to-all-start.2 = ((bf16[128,8,128]{0,2,1:T(8,128)(2,1)}), bf16[128,8,128]{0,2,1:T(8,128)(2,1)}, u32[]{:S(2)}, u32[]{:S(2)}) async-start(bf16[128,8,128]{0,2,1:T(8,128)(2,1)} %bitcast.86), calls=%async_computation.2 | async-start | bytes 524288 | tf_op jit(solution)/shard_map/all_to_all | solution.py:51
  54.7 807.2 %reduce-scatter.2.cloned.1.call-start = ((), (), s32[]{:S(2)}) async-start(), calls=%async_computation.6 | async-start | bytes 37748736 | tf_op jit(solution)/shard_map/reduce_scatter | solution.py:80
  55.3 0.6 copy-start.11
  55.3 0.6 copy-start.13
  66.8 2.0 copy-start.10
  72.4 3.3 copy-start.2
  310.9 1.4 copy-start.1
  310.9 1.4 copy-start.12
  310.9 1.4 copy-start.14
  310.9 2.0 copy-start.18
  310.9 2.0 copy-start.16
  310.9 2.0 copy-start.22
  324.6 13.8 %copy-start.21 = (f32[128]{0:T(128)S(1)}, f32[128]{0:T(128)}, u32[]{:S(2)}) copy-start(f32[128]{0:T(128)} %copy-done.20) | copy-start | bytes 1540
  332.1 9.6 %copy-start.19 = (f32[3,16,128]{2,1,0:T(8,128)S(1)}, f32[3,16,128]{2,1,0:T(8,128)}, u32[]{:S(2)}) copy-start(f32[3,16,128]{2,1,0:T(8,128)} %get-tuple-element.58) | copy-start | bytes 73732
  332.1 9.7 %copy-start.9 = (f32[4,16,128]{2,1,0:T(8,128)S(1)}, f32[4,16,128]{2,1,0:T(8,128)}, u32[]{:S(2)}) copy-start(f32[4,16,128]{2,1,0:T(8,128)} %get-tuple-element.47) | copy-start | bytes 98308
  332.8 38.3 %all-to-all-start.3 = ((bf16[8,128,128]{1,2,0:T(8,128)(2,1)}), bf16[8,128,128]{1,2,0:T(8,128)(2,1)}, u32[]{:S(2)}, u32[]{:S(2)}) async-start(bf16[8,128,128]{1,2,0:T(8,128)(2,1)} %copy.137), calls=%async_computation.3 | async-start | bytes 524288 | tf_op jit(solution)/shard_map/all_to_all | solution.py:55
  375.0 1.4 copy-start
  376.5 27.0 %collective-permute-start.1 = (f32[2,3,1024]{2,0,1:T(2,128)S(1)}, f32[2,3,1024]{2,0,1:T(2,128)S(1)}, u32[]{:S(2)}, u32[]{:S(2)}) collective-permute-start(f32[2,3,1024]{2,0,1:T(2,128)S(1)} %slice.179), channel_id=1, source_target_pairs={{4,0},{8,4},{12,8},{16,12},{20,16},{24,20},{28,24},{5,1},{9,5},{13... | collective-permute-start | bytes 73736 | tf_op jit(solution)/shard_map/ppermute | solution.py:10
  378.5 25.3 %copy-start.4 = (f32[3,1024]{1,0:T(4,128)S(1)}, f32[3,1024]{1,0:T(4,128)}, u32[]{:S(2)}) copy-start(f32[3,1024]{1,0:T(4,128)} %copy-done.3) | copy-start | bytes 36868
  378.5 25.3 %copy-start.6 = (f32[3,1024]{1,0:T(4,128)S(1)}, f32[3,1024]{1,0:T(4,128)}, u32[]{:S(2)}) copy-start(f32[3,1024]{1,0:T(4,128)} %copy-done.5) | copy-start | bytes 36868
  378.5 25.3 %copy-start.8 = (f32[3,1024]{1,0:T(4,128)S(1)}, f32[3,1024]{1,0:T(4,128)}, u32[]{:S(2)}) copy-start(f32[3,1024]{1,0:T(4,128)} %copy-done.7) | copy-start | bytes 36868
Sparse Core Ops, SparseCore 0:
  9.6 24.0 all-gather.1
  311.1 550.8 reduce-scatter.1
where the time goes:
time: 888 us; the launch traced here: 876 us
  waiting for transfers between devices  431 us (49%)
  other arithmetic  129 us (15%)
  local copies, waits for them, and re-layouts  116 us (13%)
  blocking collectives  90.1 us (10%)
  matrix products  72.8 us (8%)
  starting transfers between devices  22.1 us (2%)
  between operations  14.8 us (2%)
    reduce_scatter x1, waiting for transfers between devices, per_device(): lax.psum_scatter(lax.dot_general(cotangent, gated, (((0,), (0,)), ((), ()...  426 us
    scatter-add x1, other arithmetic, block_tables(): kernel[jnp.maximum(distance, 0)]  98.5 us
    gather x1, local copies, waits for them, and re-layouts, block_tables(): kernel[jnp.maximum(distance, 0)]  54.8 us
    psum x1, blocking collectives, per_device(): grad_taps = lax.psum(partial_taps, 'ctx')  30 us
    all_gather x1, blocking collectives, per_device(): lax.all_gather(grad_res_local, 'ctx', axis=1, tiled=True)  25.1 us
    all_gather x1, blocking collectives, per_device(): lax.all_gather(grad_rate_local, 'ctx', axis=1, tiled=True)  24 us
    dot_general x3, matrix products, long_conv(): jnp.einsum('ijc,bjc->bic', toeplitz, blocks, precision=lax.Precision.HIGH...  23.2 us
    select_n x2, local copies, waits for them, and re-layouts, block_tables(): jnp.where((distance >= 0)[:, :, None], kernel[jnp.maximum(distance, 0)],...  18.6 us
  transfers between devices with their start and end apart: 7, of which 3 were waited for; matrix products, arithmetic and copies ran while one was open for 7% of the time, Pallas kernels for 0%

commit v1 on v0

v1 whole, which is shorter than its diff:
```python
import functools

import jax
import jax.numpy as jnp
from jax import lax
from jax.experimental import pallas as pl
from jax.experimental.pallas import tpu as pltpu
from jax.sharding import PartitionSpec as P

F32 = jnp.float32
BF16 = jnp.bfloat16
LANES = 128


def shifted(value, axis, steps):
    count = lax.axis_size(axis)
    first, last = (max(0, -steps), min(count, count - steps))
    return lax.ppermute(value, axis, [(source, source + steps) for source in range(first, last)])


def rounded(value):
    return value.astype(BF16).astype(F32)


def local_states_forward(padded_ref, taps_ref, decay_ref, short_ref, state_ref):
    modes = decay_ref.shape[0]
    length = short_ref.shape[0]
    tap_count = taps_ref.shape[0]

    def filter_step(t, carry):
        for j in range(3):
            total = taps_ref[0, j] * padded_ref[t + tap_count - 1, j]
            for lag in range(1, tap_count):
                total = total + taps_ref[lag, j] * padded_ref[t + tap_count - 1 - lag, j]
            short_ref[t, j] = total
        return carry

    lax.fori_loop(0, length, filter_step, 0, unroll=4)
    decays = [decay_ref[r] for r in range(modes)]

    def step(t, states):
        product = rounded(short_ref[t, 1] * short_ref[t, 2])
        return tuple(decays[r] * states[r] + product for r in range(modes))

    zero = jnp.zeros(decay_ref.shape[1:], F32)
    final = lax.fori_loop(0, length, step, (zero,) * modes, unroll=4)
    for r in range(modes):
        state_ref[r] = final[r]


def local_states_backward(grad_conv_ref, decay_ref, state_ref):
    modes = decay_ref.shape[0]
    length = grad_conv_ref.shape[0]
    decays = [decay_ref[r] for r in range(modes)]

    def step(i, states):
        grad = grad_conv_ref[length - 1 - i]
        return tuple(decays[r] * states[r] + grad for r in range(modes))

    zero = jnp.zeros(decay_ref.shape[1:], F32)
    final = lax.fori_loop(0, length, step, (zero,) * modes, unroll=4)
    for r in range(modes):
        state_ref[r] = final[r]


def full_scans(
    padded_ref, short_ref, grad_gated_ref, grad_conv_ref, decay_ref, amp_ref, past_ref, future_ref,
    gated_ref, grad_short_ref, taps_out_ref, grad_amp_ref, grad_decay_ref,
    history, readout,
):
    modes = decay_ref.shape[0]
    length = short_ref.shape[0]
    tap_count = taps_out_ref.shape[0]
    zero = jnp.zeros(decay_ref.shape[1:], F32)
    decays = [decay_ref[r] for r in range(modes)]
    amps = [amp_ref[r] for r in range(modes)]
    for r in range(modes):
        history[0, r] = past_ref[r]

    def forward(t, states):
        product = rounded(short_ref[t, 1] * short_ref[t, 2])
        new = tuple(decays[r] * states[r] + product for r in range(modes))
        terms = [amps[r] * new[r] for r in range(modes)]
        for r in range(modes):
            history[t + 1, r] = new[r]
        while len(terms) > 1:
            terms = [terms[i] + terms[i + 1] for i in range(0, len(terms), 2)]
        convolved = rounded(terms[0])
        gated_ref[t] = short_ref[t, 0] * convolved
        grad_short_ref[t, 0] = grad_gated_ref[t] * convolved
        return new

    lax.fori_loop(0, length, forward, tuple(past_ref[r] for r in range(modes)), unroll=2)

    half = modes // 2
    for group in range(2):
        picks = list(range(group * half, group * half + half))

        def backward(i, carry):
            t = length - 1 - i
            states, grad_amp, grad_decay = carry
            grad = grad_conv_ref[t]
            new = tuple(decays[r] * states[k] + grad for k, r in enumerate(picks))
            terms = [amps[r] * new[k] for k, r in enumerate(picks)]
            grad_amp = tuple(grad_amp[k] + grad * history[t + 1, r] for k, r in enumerate(picks))
            grad_decay = tuple(grad_decay[k] + new[k] * history[t, r] for k, r in enumerate(picks))
            while len(terms) > 1:
                terms = [terms[i] + terms[i + 1] for i in range(0, len(terms), 2)]
            if group == 0:
                readout[t] = terms[0]
            else:
                grad_product = rounded(readout[t] + terms[0])
                grad_short_ref[t, 1] = grad_product * short_ref[t, 2]
                grad_short_ref[t, 2] = grad_product * short_ref[t, 1]
            return new, grad_amp, grad_decay

        start = (tuple(future_ref[r] for r in picks), (zero,) * half, (zero,) * half)
        unused, grad_amp, grad_decay = lax.fori_loop(0, length, backward, start, unroll=2)
        for k, r in enumerate(picks):
            grad_amp_ref[r] = grad_amp[k]
            grad_decay_ref[r] = grad_decay[k]

    def taps_step(t, sums):
        new = []
        for j in range(3):
            grad = grad_short_ref[t, j]
            for lag in range(tap_count):
                new.append(sums[j * tap_count + lag] + grad * padded_ref[t + tap_count - 1 - lag, j])
        return tuple(new)

    sums = lax.fori_loop(0, length, taps_step, (zero,) * (3 * tap_count), unroll=4)
    for j in range(3):
        for lag in range(tap_count):
            taps_out_ref[lag, j] = sums[j * tap_count + lag]


def call(kernel, outs, scratch=(), mib=48):
    return pl.pallas_call(
        kernel,
        out_shape=[jax.ShapeDtypeStruct(shape, F32) for shape in outs],
        scratch_shapes=[pltpu.VMEM(shape, F32) for shape in scratch],
        compiler_params=pltpu.CompilerParams(vmem_limit_bytes=mib * 2**20),
    )


def per_device(features, short_taps, residues, log_rate, out_weight, grad_out):
    length, triple, width = features.shape
    tap_count = short_taps.shape[0]
    modes = residues.shape[0]
    groups = lax.axis_size("ctx")
    ranks = lax.axis_size("tp")
    position = lax.axis_index("ctx")
    rank = lax.axis_index("tp")
    rows = width // LANES
    tile = (rows, LANES)

    cotangent = lax.all_gather(grad_out, "tp", axis=1, tiled=True)
    rim_rows = shifted(features[length - (tap_count - 1) :], "ctx", 1)
    padded = jnp.concatenate([rim_rows, features], axis=0).astype(F32)
    padded = padded.reshape((length + tap_count - 1, triple) + tile)
    taps = short_taps.reshape((tap_count, triple) + tile)
    half_rate = jnp.exp(0.5 * log_rate).reshape((modes,) + tile)
    rate = jnp.exp(log_rate).reshape((modes,) + tile)
    amp = residues.reshape((modes,) + tile) * half_rate
    decay = jnp.exp(-rate)
    block_decay = jnp.exp(-rate * length)

    short, past_local = call(
        local_states_forward, [(length, triple) + tile, (modes,) + tile]
    )(padded, taps, decay)

    grad_gated = lax.dot_general(
        cotangent, out_weight, (((1,), (1,)), ((), ())), preferred_element_type=F32
    ).reshape((length,) + tile)
    grad_conv = rounded(grad_gated * short[:, 0])
    (future_local,) = call(local_states_backward, [(modes,) + tile])(grad_conv, decay)

    states = lax.all_gather(jnp.stack([past_local, future_local]), "ctx", axis=0)
    past = jnp.zeros((modes,) + tile, F32)
    future = past
    for block in range(groups - 1):
        past = jnp.where(block < position, block_decay * past + states[block, 0], past)
    for block in range(groups - 1, 0, -1):
        future = jnp.where(block > position, block_decay * future + states[block, 1], future)

    features_out = cotangent.shape[1]
    share = features_out // (groups * ranks)
    mine = lax.dynamic_index_in_dim(
        cotangent.reshape(length, groups, ranks, share), rank, 2, keepdims=False
    )
    swapped = lax.all_to_all(
        mine.reshape(length, groups * share), "ctx", split_axis=1, concat_axis=0, tiled=True
    )
    block_cotangent = lax.all_gather(swapped, "tp", axis=1, tiled=True)

    gated, grad_short, part_taps, grad_amp, grad_decay = call(
        full_scans,
        [(length,) + tile, (length, triple) + tile, (tap_count, triple) + tile]
        + [(modes,) + tile] * 2,
        [(length + 1, modes) + tile, (length,) + tile],
    )(padded, short, grad_gated, grad_conv, decay, amp, past, future)

    gated_all = lax.all_gather(
        gated.astype(BF16).reshape(length, width), "ctx", axis=0, tiled=True
    )
    grad_weight_t = lax.dot_general(
        block_cotangent, gated_all, (((0,), (0,)), ((), ())), preferred_element_type=F32
    )

    tail_rows = shifted(grad_short[: tap_count - 1], "ctx", -1)
    tail_pad = jnp.concatenate([grad_short, tail_rows], axis=0)
    grad_features = sum(taps[lag] * tail_pad[lag : lag + length] for lag in range(tap_count))
    packed = jnp.concatenate(
        [part_taps.reshape((tap_count * triple,) + tile), grad_amp, grad_decay], axis=0
    )
    total = lax.psum(packed, "ctx")
    grad_taps = total[: tap_count * triple].reshape(tap_count, triple, width)
    grad_amp = total[tap_count * triple : tap_count * triple + modes]
    grad_decay = total[tap_count * triple + modes :]
    grad_residues = (grad_amp * half_rate).reshape(modes, width)
    grad_log_rate = (0.5 * grad_amp * amp - grad_decay * amp * decay * rate).reshape(modes, width)
    return (
        grad_features.astype(BF16).reshape(length, triple, width),
        grad_taps,
        grad_residues,
        grad_log_rate,
        grad_weight_t,
    )


def solution(mesh):
    return jax.shard_map(
        per_device,
        mesh=mesh,
        in_specs=(
            P("ctx", None, "tp"),
            P(None, None, "tp"),
            P(None, "tp"),
            P(None, "tp"),
            P("tp", None),
            P("ctx", "tp"),
        ),
        out_specs=(
            P("ctx", None, "tp"),
            P(None, None, "tp"),
            P(None, "tp"),
            P(None, "tp"),
            P("ctx", "tp"),
        ),
        check_vma=False,
    )
```

time: 888 us -> 264 us (0.30)
  waiting for transfers between devices: 431 us -> 187 us
  other arithmetic: 129 us -> 6.12 us
  local copies, waits for them, and re-layouts: 116 us -> 13.2 us
  blocking collectives: 90.1 us -> 0 us
  matrix products: 72.8 us -> 18.7 us
  starting transfers between devices: 22.1 us -> 11.9 us
    reduce_scatter x1 -> x0, waiting for transfers between devices: 426 us -> none  [per_device(): lax.psum_scatter(lax.dot_general(cotangent, gated, (((0,), (0,)), ((), ()...]
    all_gather x0 -> x3, waiting for transfers between devices: none -> 107 us  [the longest x1 49.9 us: per_device(): lax.all_gather(gated.astype(BF16).reshape(length, width), 'ctx', axis=0,...]
    scatter-add x1 -> x0, other arithmetic: 98.5 us -> none  [block_tables(): kernel[jnp.maximum(distance, 0)]]
    psum x0 -> x1, waiting for transfers between devices: none -> 59.7 us  [per_device(): total = lax.psum(packed, 'ctx')]
    gather x1 -> x0, local copies, waits for them, and re-layouts: 54.8 us -> none  [block_tables(): kernel[jnp.maximum(distance, 0)]]
    dot_general x10 -> x1, matrix products: 59.9 us -> 6.62 us  [per_device(): lax.dot_general(block_cotangent, gated_all, (((0,), (0,)), ((), ())), pre...]
    all_gather x2 -> x0, blocking collectives: 49.1 us -> none  [the longest x1 25.1 us: per_device(): lax.all_gather(grad_res_local, 'ctx', axis=1, tiled=True)]
    psum x1 -> x0, blocking collectives: 30 us -> none  [per_device(): grad_taps = lax.psum(partial_taps, 'ctx')]
  transfers between devices with their start and end apart: 7 -> 8, of which waited for: 3 -> 7; matrix products, arithmetic and copies ran while one was open for 7% -> 5% of each run, Pallas kernels for 0% -> 3%
where the time goes in v1:
time: 264 us; the launch traced here: 260 us
  waiting for transfers between devices  187 us (71%)
  matrix products  18.7 us (7%)
  between operations  14.1 us (5%)
  local copies, waits for them, and re-layouts  13.2 us (5%)
  starting transfers between devices  11.9 us (5%)
  Pallas kernels  8.75 us (3%)
  other arithmetic  6.12 us (2%)
    psum x1, waiting for transfers between devices, per_device(): total = lax.psum(packed, 'ctx')  59.7 us
    all_gather x1, waiting for transfers between devices, per_device(): lax.all_gather(gated.astype(BF16).reshape(length, width), 'ctx', axis=0,...  49.9 us
    all_gather x1, waiting for transfers between devices, per_device(): lax.all_gather(jnp.stack([past_local, future_local]), 'ctx', axis=0)  33.1 us
    all_gather x1, waiting for transfers between devices, per_device(): block_cotangent = lax.all_gather(swapped, 'tp', axis=1, tiled=True)  23.7 us
    all_gather x1, waiting for transfers between devices, per_device(): cotangent = lax.all_gather(grad_out, 'tp', axis=1, tiled=True)  17.2 us
    dot_general x1, matrix products, per_device(): lax.dot_general(cotangent, out_weight, (((1,), (1,)), ((), ())), preferre...  12.1 us
    unnamed x25, local copies, waits for them, and re-layouts  7.21 us
    pallas_call x1, Pallas kernels, per_device(): call(full_scans, [(length,) + tile, (length, triple) + tile, (tap_count,...  6.97 us
  transfers between devices with their start and end apart: 8, of which 7 were waited for; matrix products, arithmetic and copies ran while one was open for 5% of the time, Pallas kernels for 3%

profile of v1, /device:TPU:13, one launch (start us, length us, event | category | flops | bytes accessed | tf_op | source)
XLA Modules:
  0.0 259.5 jit_solution(15668277584214571199)
XLA Ops:
  7.2 0.0 all-gather.6.cloned.1.call-start
  7.2 2.1 copy.34
  9.3 0.0 all-gather.6.cloned.1.call-update
  9.4 0.0 all-gather.12.cloned.1.call-start
  9.4 0.8 slice.79
  10.2 3.1 %collective-permute-start = (bf16[2,3,1024]{2,0,1:T(2,128)(2,1)S(1)}, bf16[2,3,1024]{2,0,1:T(2,128)(2,1)S(1)}, u32[]{:S(2)}, u32[]{:S(2)}) collective-permute-start(bf16[2,3,1024]{2,0,1:T(2,128)(2,1)S(1)} %slice.79), channel_id=1, source_target_pairs={{0,4},{4,8},{8,12},{12,16},{16,20},{20,24},{24,28},{1,5},{5,9},{9,... | collective-permute-start | bytes 36872 | tf_op jit(solution)/shard_map/ppermute | solution.py:18
  13.5 0.4 copy.31
  13.9 0.4 copy.33
  14.4 0.3 collective-permute-done
  14.7 0.1 maximum_convert_fusion.padded_ref
  14.8 1.2 shard_map.101
  16.0 1.1 copy-done.1
  17.1 17.2 %all-gather.6.cloned.1.call-done = bf16[128,8192]{0,1:T(8,128)(2,1)} async-done(((bf16[128,2048]{0,1:T(8,128)(2,1)}), bf16[128,8192]{0,1:T(8,128)(2,1)}) %all-gather.6.cloned.1.call-update) | async-done | bytes 2097168 | tf_op jit(solution)/shard_map/all_gather | solution.py:157
  34.3 12.1 %convolution_bitcast_fusion = f32[16,8,8,128]{3,1,2,0:T(8,128)S(1)} fusion(bf16[128,8192]{0,1:T(8,128)(2,1)} %all-gather.6.cloned.1.call-done, bf16[1024,8192]{1,0:T(8,128)(2,1)} %param.10), kind=kOutput, calls=%fused_computation.5 | convolution fusion | flops 2147483648 | bytes 19398656 | tf_op jit(solution)/shard_map/dot_general | solution.py:172
  46.4 0.1 copy.44
  46.5 1.1 fusion.5.grad_conv_ref
  47.7 0.6 shard_map.102
  48.3 0.7 pad_maximum_fusion.1
  49.0 0.0 all-gather.12.cloned.1.call-update
  49.1 1.1 dynamic-slice_bitcast_fusion
  50.2 1.0 copy.38
  51.2 5.5 %all-to-all-start = ((bf16[128,8,256]{2,0,1:T(8,128)(2,1)}), bf16[128,8,256]{2,0,1:T(8,128)(2,1)}, u32[]{:S(2)}, u32[]{:S(2)}) async-start(bf16[128,8,256]{2,0,1:T(8,128)(2,1)} %copy.38), calls=%async_computation | async-start | bytes 1048576 | tf_op jit(solution)/shard_map/all_to_all | solution.py:191
  56.7 33.1 %all-gather.12.cloned.1.call-done = f32[16,16,8,128]{3,2,1,0:T(8,128)} async-done(((f32[2,16,8,128]{3,2,1,0:T(8,128)}), f32[16,16,8,128]{3,2,1,0:T(8,128)}) %all-gather.12.cloned.1.call-update) | async-done | bytes 1048592 | tf_op jit(solution)/shard_map/all_gather | solution.py:178
  89.8 1.1 fusion.23.past_ref
  90.9 1.1 fusion.9.future_ref
  92.1 1.4 copy-done.2
  93.5 7.0 %shard_map.103 = (f32[128,8,128]{2,1,0:T(8,128)S(1)}, f32[128,3,8,128]{3,2,1,0:T(8,128)S(1)}, f32[3,3,8,128]{3,2,1,0:T(8,128)S(1)}, f32[16,8,128]{2,1,0:T(8,128)S(1)}, f32[16,8,128]{2,1,0:T(8,128)S(1)}) custom-call(f32[130,3,8,128]{3,2,1,0:T(8,128)} %copy-done, f32[128,3,8,128]{3,2,1,0:T(8,128)S(1)} %copy-done.2, f32[128,8,128]{2,1,0:T(8,128)S(1)} %bitcast.189, ...), custom_call_target="tpu_custom_call" | custom-call | tf_op jit(solution)/shard_map/pallas_call | solution.py:196
  100.4 0.7 pad_maximum_fusion
  101.1 0.0 all-reduce.2.cloned.1.call-update
  101.2 0.0 all-gather.8.cloned.1.call-start
  101.2 0.5 all-gather.8.cloned.1.call-update
  101.7 0.0 all-gather.10.cloned.1.call-start
  101.8 0.8 copy.62
  102.6 0.0 all-gather.10.cloned.1.call-update
  102.7 3.1 %collective-permute-start.1 = (f32[2,3,8,128]{3,2,1,0:T(8,128)S(1)}, f32[2,3,8,128]{3,2,1,0:T(8,128)S(1)}, u32[]{:S(2)}, u32[]{:S(2)}) collective-permute-start(f32[2,3,8,128]{3,2,1,0:T(8,128)S(1)} %slice.96), channel_id=1, source_target_pairs={{4,0},{8,4},{12,8},{16,12},{20,16},{24,20},{28,24},{5,1},{9,5},{13... | collective-permute-start | bytes 73736 | tf_op jit(solution)/shard_map/ppermute | solution.py:18
  105.8 0.1 constant_dynamic-update-slice_fusion.1
  105.9 2.2 collective-permute-done.1
  108.1 0.3 fusion.1
  108.5 0.5 copy.36
  109.0 1.2 copy.39
  110.2 59.7 %all-reduce.2.cloned.1.call-done = f32[41,8,128]{2,1,0:T(8,128)} async-done(((f32[41,8,128]{2,1,0:T(8,128)}), f32[41,8,128]{2,1,0:T(8,128)}) %all-reduce.2.cloned.1.call-update) | async-done | bytes 167952 | tf_op jit(solution)/shard_map/psum | solution.py:216
  169.9 0.8 slice.120
  170.6 0.6 reshape.68
  171.3 0.9 fusion.6
  172.2 0.7 copy_bitcast_fusion.1
  172.8 23.7 %all-gather.8.cloned.1.call-done = bf16[1024,1024]{1,0:T(8,128)(2,1)} async-done(((bf16[1024,256]{1,0:T(8,128)(2,1)}), bf16[1024,1024]{1,0:T(8,128)(2,1)}) %all-gather.8.cloned.1.call-update) | async-done | bytes 2097168 | tf_op jit(solution)/shard_map/all_gather | solution.py:194
  196.5 49.9 %all-gather.10.cloned.1.call-done = bf16[1024,1024]{1,0:T(8,128)(2,1)} async-done(((bf16[128,1024]{1,0:T(8,128)(2,1)}), bf16[1024,1024]{1,0:T(8,128)(2,1)}) %all-gather.10.cloned.1.call-update) | async-done | bytes 2097168 | tf_op jit(solution)/shard_map/all_gather | solution.py:203
  246.4 6.6 %fusion.37 = f32[1024,1024]{1,0:T(8,128)} fusion(bf16[1024,1024]{1,0:T(8,128)(2,1)} %all-gather.8.cloned.1.call-done, bf16[1024,1024]{1,0:T(8,128)(2,1)} %all-gather.10.cloned.1.call-done), kind=kOutput, calls=%fused_computation.78 | convolution fusion | flops 2147483648 | bytes 8388608 | tf_op jit(solution)/shard_map/dot_general | solution.py:206
  (28 shorter events, 0.2 us)
Async XLA Ops:
  7.2 6.3 %copy-start.3 = (bf16[128,3,1024]{2,0,1:T(8,128)(2,1)S(1)}, bf16[128,3,1024]{2,0,1:T(8,128)(2,1)}, u32[]{:S(2)}) copy-start(bf16[128,3,1024]{2,0,1:T(8,128)(2,1)} %param.6) | copy-start | bytes 2359300
  7.2 6.2 %copy-start.5 = (f32[16,1024]{1,0:T(8,128)S(1)}, f32[16,1024]{1,0:T(8,128)}, u32[]{:S(2)}) copy-start(f32[16,1024]{1,0:T(8,128)} %param.9) | copy-start | bytes 196612
  7.2 27.1 %all-gather.6.cloned.1.call-start = ((), (), s32[]{:S(2)}) async-start(), calls=%async_computation.1 | async-start | bytes 2621440 | tf_op jit(solution)/shard_map/all_gather | solution.py:157
  9.4 80.5 %all-gather.12.cloned.1.call-start = ((), (), s32[]{:S(2)}) async-start(), calls=%async_computation.5 | async-start | bytes 1179648 | tf_op jit(solution)/shard_map/all_gather | solution.py:178
  10.2 4.4 %collective-permute-start = (bf16[2,3,1024]{2,0,1:T(2,128)(2,1)S(1)}, bf16[2,3,1024]{2,0,1:T(2,128)(2,1)S(1)}, u32[]{:S(2)}, u32[]{:S(2)}) collective-permute-start(bf16[2,3,1024]{2,0,1:T(2,128)(2,1)S(1)} %slice.79), channel_id=1, source_target_pairs={{0,4},{4,8},{8,12},{12,16},{16,20},{20,24},{24,28},{1,5},{5,9},{9,... | collective-permute-start | bytes 36872 | tf_op jit(solution)/shard_map/ppermute | solution.py:18
  13.5 0.8 copy-start.4
  14.8 31.6 %copy-start = (f32[130,3,8,128]{3,2,1,0:T(8,128)}, f32[130,3,8,128]{3,2,1,0:T(8,128)S(1)}, u32[]{:S(2)}) copy-start(f32[130,3,8,128]{3,2,1,0:T(8,128)S(1)} %maximum_convert_fusion.padded_ref) | copy-start | bytes 4792324
  16.0 1.1 copy-start.1
  46.5 2.5 copy-start.6
  51.2 50.0 %all-to-all-start = ((bf16[128,8,256]{2,0,1:T(8,128)(2,1)}), bf16[128,8,256]{2,0,1:T(8,128)(2,1)}, u32[]{:S(2)}, u32[]{:S(2)}) async-start(bf16[128,8,256]{2,0,1:T(8,128)(2,1)} %copy.38), calls=%async_computation | async-start | bytes 1048576 | tf_op jit(solution)/shard_map/all_to_all | solution.py:191
  56.7 113.2 %all-reduce.2.cloned.1.call-start = ((), (), s32[]{:S(2)}) async-start(), calls=%async_computation.2 | async-start | bytes 335872 | tf_op jit(solution)/shard_map/psum | solution.py:216
  92.1 1.4 copy-start.2
  101.2 95.3 %all-gather.8.cloned.1.call-start = ((), (), s32[]{:S(2)}) async-start(), calls=%async_computation.3 | async-start | bytes 2621440 | tf_op jit(solution)/shard_map/all_gather | solution.py:194
  101.7 144.7 %all-gather.10.cloned.1.call-start = ((), (), s32[]{:S(2)}) async-start(), calls=%async_computation.4 | async-start | bytes 2359296 | tf_op jit(solution)/shard_map/all_gather | solution.py:203
  102.7 5.5 %collective-permute-start.1 = (f32[2,3,8,128]{3,2,1,0:T(8,128)S(1)}, f32[2,3,8,128]{3,2,1,0:T(8,128)S(1)}, u32[]{:S(2)}, u32[]{:S(2)}) collective-permute-start(f32[2,3,8,128]{3,2,1,0:T(8,128)S(1)} %slice.96), channel_id=1, source_target_pairs={{4,0},{8,4},{12,8},{16,12},{20,16},{24,20},{28,24},{5,1},{9,5},{13... | collective-permute-start | bytes 73736 | tf_op jit(solution)/shard_map/ppermute | solution.py:18
Sparse Core Ops, SparseCore 0:
  10.2 24.0 all-gather.5
  49.1 40.6 all-gather.11
  101.3 68.5 all-reduce.1
  171.3 25.1 all-gather.7
  199.3 47.0 all-gather.9

commit v2 on v1

v2 whole, which is shorter than its diff:
```python
import jax
import jax.numpy as jnp
from jax import lax
from jax.experimental import pallas as pl
from jax.experimental.pallas import tpu as pltpu
from jax.sharding import PartitionSpec as P

F32 = jnp.float32
BF16 = jnp.bfloat16
LANES = 128


def shifted(value, axis, steps):
    count = lax.axis_size(axis)
    first, last = (max(0, -steps), min(count, count - steps))
    return lax.ppermute(value, axis, [(source, source + steps) for source in range(first, last)])


def rounded(value):
    return value.astype(BF16).astype(F32)


def peer(offset):
    count = lax.axis_size("ctx")
    return lax.rem(lax.axis_index("ctx") + offset + count, count)


def greet():
    barrier = pltpu.get_barrier_semaphore()
    for offset in range(1, lax.axis_size("ctx")):
        pl.semaphore_signal(
            barrier, inc=1, device_id={"ctx": peer(offset)}, device_id_type=pl.DeviceIdType.MESH
        )


def await_greetings():
    pl.semaphore_wait(pltpu.get_barrier_semaphore(), lax.axis_size("ctx") - 1)


def push(source, target, send_sem, recv_sem, offset):
    copy = pltpu.make_async_remote_copy(
        src_ref=source,
        dst_ref=target,
        send_sem=send_sem,
        recv_sem=recv_sem,
        device_id={"ctx": peer(offset)},
        device_id_type=pl.DeviceIdType.MESH,
    )
    copy.start()
    return copy


def tree_sum(terms):
    while len(terms) > 1:
        pairs = [terms[i] + terms[i + 1] for i in range(0, len(terms) - 1, 2)]
        terms = pairs + terms[len(terms) - len(terms) % 2 :]
    return terms[0]


def forward_kernel(
    padded_ref, taps_ref, decay_ref, block_decay_ref, amp_ref,
    short_ref, gated_ref, convolved_ref, past_ref,
    own, arrived, send_sems, recv_sems,
):
    modes = decay_ref.shape[0]
    length = short_ref.shape[0]
    tap_count = taps_ref.shape[0]
    count = lax.axis_size("ctx")
    position = lax.axis_index("ctx")
    greet()

    def filter_step(t, carry):
        for j in range(3):
            total = taps_ref[0, j] * padded_ref[t + tap_count - 1, j]
            for lag in range(1, tap_count):
                total = total + taps_ref[lag, j] * padded_ref[t + tap_count - 1 - lag, j]
            short_ref[t, j] = total
        return carry

    lax.fori_loop(0, length, filter_step, 0, unroll=4)
    decays = [decay_ref[r] for r in range(modes)]
    zero = jnp.zeros(decay_ref.shape[1:], F32)

    def local_step(t, states):
        product = rounded(short_ref[t, 1] * short_ref[t, 2])
        return tuple(decays[r] * states[r] + product for r in range(modes))

    final = lax.fori_loop(0, length, local_step, (zero,) * modes, unroll=4)
    for r in range(modes):
        own[r] = final[r]

    await_greetings()
    copies = [
        push(own, arrived.at[position], send_sems.at[k], recv_sems.at[k], k)
        for k in range(1, count)
    ]
    arrived[position] = own[...]
    for copy in copies:
        copy.wait()
    past_ref[...] = jnp.zeros(past_ref.shape, F32)
    for block in range(count - 1):
        past_ref[...] = jnp.where(
            block < position, block_decay_ref[...] * past_ref[...] + arrived[block], past_ref[...]
        )

    def step(t, states):
        product = rounded(short_ref[t, 1] * short_ref[t, 2])
        new = tuple(decays[r] * states[r] + product for r in range(modes))
        convolved = rounded(tree_sum([amp_ref[r] * new[r] for r in range(modes)]))
        convolved_ref[t] = convolved
        gated_ref[t] = short_ref[t, 0] * convolved
        return new

    lax.fori_loop(0, length, step, tuple(past_ref[r] for r in range(modes)), unroll=2)


def backward_kernel(
    padded_ref, short_ref, convolved_ref, grad_gated_ref, taps_ref, decay_ref, block_decay_ref,
    amp_ref, past_ref,
    grad_features_ref, total_ref,
    own, arrived, future, history, grad_conv, grad_short, readout, tail, packed, pieces, summed,
    state_send, state_recv, piece_send, piece_recv, sum_send, sum_recv, tail_send, tail_recv,
):
    modes = decay_ref.shape[0]
    length = short_ref.shape[0]
    tap_count = taps_ref.shape[0]
    share = summed.shape[0]
    count = lax.axis_size("ctx")
    position = lax.axis_index("ctx")
    zero = jnp.zeros(decay_ref.shape[1:], F32)
    decays = [decay_ref[r] for r in range(modes)]
    greet()

    def local_step(i, states):
        t = length - 1 - i
        grad = rounded(grad_gated_ref[t] * short_ref[t, 0])
        grad_conv[t] = grad
        return tuple(decays[r] * states[r] + grad for r in range(modes))

    final = lax.fori_loop(0, length, local_step, (zero,) * modes, unroll=4)
    for r in range(modes):
        own[r] = final[r]
    await_greetings()
    copies = [
        push(own, arrived.at[position], state_send.at[k], state_recv.at[k], k)
        for k in range(1, count)
    ]
    arrived[position] = own[...]

    for r in range(modes):
        history[0, r] = past_ref[r]

    def forward(t, states):
        product = rounded(short_ref[t, 1] * short_ref[t, 2])
        new = tuple(decays[r] * states[r] + product for r in range(modes))
        for r in range(modes):
            history[t + 1, r] = new[r]
        grad_short[t, 0] = grad_gated_ref[t] * convolved_ref[t]
        return new

    lax.fori_loop(0, length, forward, tuple(past_ref[r] for r in range(modes)), unroll=2)

    for copy in copies:
        copy.wait()
    future[...] = jnp.zeros(future.shape, F32)
    for block in range(count - 1, 0, -1):
        future[...] = jnp.where(
            block > position, block_decay_ref[...] * future[...] + arrived[block], future[...]
        )

    half = modes // 2
    base = 3 * tap_count
    for group in range(2):
        picks = list(range(group * half, group * half + half))

        def backward(i, carry):
            t = length - 1 - i
            states, grad_amp, grad_decay = carry
            grad = grad_conv[t]
            new = tuple(decays[r] * states[k] + grad for k, r in enumerate(picks))
            term = tree_sum([amp_ref[r] * new[k] for k, r in enumerate(picks)])
            grad_amp = tuple(grad_amp[k] + grad * history[t + 1, r] for k, r in enumerate(picks))
            grad_decay = tuple(grad_decay[k] + new[k] * history[t, r] for k, r in enumerate(picks))
            if group == 0:
                readout[t] = term
            else:
                grad_product = rounded(readout[t] + term)
                grad_short[t, 1] = grad_product * short_ref[t, 2]
                grad_short[t, 2] = grad_product * short_ref[t, 1]
            return new, grad_amp, grad_decay

        start = (tuple(future[r] for r in picks), (zero,) * half, (zero,) * half)
        unused, grad_amp, grad_decay = lax.fori_loop(0, length, backward, start, unroll=2)
        for k, r in enumerate(picks):
            packed[base + r] = grad_amp[k]
            packed[base + modes + r] = grad_decay[k]

    tail_copy = push(
        grad_short.at[pl.ds(0, tap_count - 1)], tail, tail_send.at[0], tail_recv.at[0], -1
    )

    def taps_step(t, sums):
        new = []
        for j in range(3):
            grad = grad_short[t, j]
            for lag in range(tap_count):
                new.append(sums[j * tap_count + lag] + grad * padded_ref[t + tap_count - 1 - lag, j])
        return tuple(new)

    sums = lax.fori_loop(0, length, taps_step, (zero,) * base, unroll=4)
    for j in range(3):
        for lag in range(tap_count):
            packed[lag * 3 + j] = sums[j * tap_count + lag]
    for extra in range(base + 2 * modes, packed.shape[0]):
        packed[extra] = zero

    copies = [
        push(
            packed.at[pl.ds(peer(k) * share, share)], pieces.at[position],
            piece_send.at[k], piece_recv.at[k], k,
        )
        for k in range(1, count)
    ]
    pieces[position] = packed[pl.ds(position * share, share)]

    def features_step(t, carry):
        for j in range(3):
            total = taps_ref[0, j] * grad_short[t, j]
            for lag in range(1, tap_count):
                total = total + taps_ref[lag, j] * grad_short[t + lag, j]
            grad_features_ref[t, j] = total
        return carry

    lax.fori_loop(0, length - tap_count + 1, features_step, 0, unroll=2)

    for copy in copies:
        copy.wait()
    summed[...] = tree_sum([pieces[block] for block in range(count)])
    copies = [
        push(
            summed, total_ref.at[pl.ds(position * share, share)],
            sum_send.at[k], sum_recv.at[k], k,
        )
        for k in range(1, count)
    ]
    total_ref[pl.ds(position * share, share)] = summed[...]

    tail_copy.wait()
    inner = position < count - 1
    for t in range(length - tap_count + 1, length):
        for j in range(3):
            total = taps_ref[0, j] * grad_short[t, j]
            for lag in range(1, tap_count):
                if t + lag < length:
                    later = grad_short[t + lag, j]
                else:
                    later = jnp.where(inner, tail[t + lag - length, j], 0.0)
                total = total + taps_ref[lag, j] * later
            grad_features_ref[t, j] = total
    for copy in copies:
        copy.wait()


def call(kernel, outs, scratch, identity, mib=48):
    return pl.pallas_call(
        kernel,
        out_shape=[jax.ShapeDtypeStruct(shape, F32) for shape in outs],
        scratch_shapes=[
            pltpu.SemaphoreType.DMA((item,)) if isinstance(item, int) else pltpu.VMEM(item, F32)
            for item in scratch
        ],
        compiler_params=pltpu.CompilerParams(
            vmem_limit_bytes=mib * 2**20, collective_id=identity, has_side_effects=True
        ),
    )


def per_device(features, short_taps, residues, log_rate, out_weight, grad_out):
    length, triple, width = features.shape
    tap_count = short_taps.shape[0]
    modes = residues.shape[0]
    groups = lax.axis_size("ctx")
    ranks = lax.axis_size("tp")
    rank = lax.axis_index("tp")
    rows = width // LANES
    tile = (rows, LANES)
    state = (modes,) + tile

    cotangent = lax.all_gather(grad_out, "tp", axis=1, tiled=True)
    rim_rows = shifted(features[length - (tap_count - 1) :], "ctx", 1)
    padded = jnp.concatenate([rim_rows, features], axis=0).astype(F32)
    padded = padded.reshape((length + tap_count - 1, triple) + tile)
    taps = short_taps.reshape((tap_count, triple) + tile)
    half_rate = jnp.exp(0.5 * log_rate).reshape(state)
    rate = jnp.exp(log_rate).reshape(state)
    amp = residues.reshape(state) * half_rate
    decay = jnp.exp(-rate)
    block_decay = jnp.exp(-rate * length)

    short, gated, convolved, past = call(
        forward_kernel,
        [(length, triple) + tile, (length,) + tile, (length,) + tile, state],
        [state, (groups,) + state, groups, groups],
        0,
    )(padded, taps, decay, block_decay, amp)
    gated_all = lax.all_gather(
        gated.astype(BF16).reshape(length, width), "ctx", axis=0, tiled=True
    )

    grad_gated = lax.dot_general(
        cotangent, out_weight, (((1,), (1,)), ((), ())), preferred_element_type=F32
    ).reshape((length,) + tile)

    features_out = cotangent.shape[1]
    portion = features_out // (groups * ranks)
    mine = lax.dynamic_index_in_dim(
        cotangent.reshape(length, groups, ranks, portion), rank, 2, keepdims=False
    )
    swapped = lax.all_to_all(
        mine.reshape(length, groups * portion), "ctx", split_axis=1, concat_axis=0, tiled=True
    )
    block_cotangent = lax.all_gather(swapped, "tp", axis=1, tiled=True)

    base = tap_count * triple
    share = -(-(base + 2 * modes) // groups)
    grad_features, total = call(
        backward_kernel,
        [(length, triple) + tile, (groups * share,) + tile],
        [
            state, (groups,) + state, state, (length + 1,) + state, (length,) + tile,
            (length, triple) + tile, (length,) + tile, (tap_count - 1, triple) + tile,
            (groups * share,) + tile, (groups, share) + tile, (share,) + tile,
            groups, groups, groups, groups, groups, groups, 1, 1,
        ],
        1,
    )(padded, short, convolved, grad_gated, taps, decay, block_decay, amp, past)

    grad_weight_t = lax.dot_general(
        block_cotangent, gated_all, (((0,), (0,)), ((), ())), preferred_element_type=F32
    )
    grad_taps = total[:base].reshape(tap_count, triple, width)
    grad_amp = total[base : base + modes]
    grad_decay = total[base + modes : base + 2 * modes]
    grad_residues = (grad_amp * half_rate).reshape(modes, width)
    grad_log_rate = (0.5 * grad_amp * amp - grad_decay * amp * decay * rate).reshape(modes, width)
    return (
        grad_features.astype(BF16).reshape(length, triple, width),
        grad_taps,
        grad_residues,
        grad_log_rate,
        grad_weight_t,
    )


def solution(mesh):
    return jax.shard_map(
        per_device,
        mesh=mesh,
        in_specs=(
            P("ctx", None, "tp"),
            P(None, None, "tp"),
            P(None, "tp"),
            P(None, "tp"),
            P("tp", None),
            P("ctx", "tp"),
        ),
        out_specs=(
            P("ctx", None, "tp"),
            P(None, None, "tp"),
            P(None, "tp"),
            P(None, "tp"),
            P("ctx", "tp"),
        ),
        check_vma=False,
    )
```

time: 264 us -> 141 us (0.53)
  waiting for transfers between devices: 187 us -> 8.3 us
  Pallas kernels: 8.75 us -> 56.1 us
  blocking collectives: 0 us -> 23.4 us
  starting transfers between devices: 11.9 us -> 3.27 us
  other arithmetic: 6.12 us -> 1.17 us
    psum x1 -> x0, waiting for transfers between devices: 59.7 us -> none  [per_device(): total = lax.psum(packed, 'ctx')]
    all_gather x1, waiting for transfers between devices: 49.9 us -> 0.01 us  [per_device(): lax.all_gather(gated.astype(BF16).reshape(length, width), 'ctx', axis=0,...]
    pallas_call x3 -> x2, Pallas kernels: 8.75 us -> 56.1 us  [the longest x1 39 us: per_device(): call(backward_kernel, [(length, triple) + tile, (groups * share,) + tile]...]
    all_gather x1 -> x0, waiting for transfers between devices: 33.1 us -> none  [per_device(): lax.all_gather(jnp.stack([past_local, future_local]), 'ctx', axis=0)]
    all_to_all x0 -> x1, blocking collectives: none -> 23.4 us  [per_device(): lax.all_to_all(mine.reshape(length, groups * portion), 'ctx', split_axis=...]
    all_gather x1, waiting for transfers between devices: 17.2 us -> 0.02 us  [per_device(): cotangent = lax.all_gather(grad_out, 'tp', axis=1, tiled=True)]
    all_gather x1, waiting for transfers between devices: 23.7 us -> 8.23 us  [per_device(): block_cotangent = lax.all_gather(swapped, 'tp', axis=1, tiled=True)]
    all_to_all x1 -> x0, starting transfers between devices: 5.48 us -> none  [per_device(): lax.all_to_all(mine.reshape(length, groups * share), 'ctx', split_axis=1,...]
  transfers between devices with their start and end apart: 8 -> 4, of which waited for: 7 -> 1; matrix products, arithmetic and copies ran while one was open for 5% -> 17% of each run, Pallas kernels for 3% -> 40%
where the time goes in v2:
time: 141 us; the launch traced here: 139 us
  Pallas kernels  56.1 us (40%)
  blocking collectives  23.4 us (17%)
  matrix products  18.8 us (13%)
  local copies, waits for them, and re-layouts  14 us (10%)
  between operations  14 us (10%)
  waiting for transfers between devices  8.3 us (6%)
  starting transfers between devices  3.27 us (2%)
    pallas_call x1, Pallas kernels, per_device(): call(backward_kernel, [(length, triple) + tile, (groups * share,) + tile]...  39 us
    all_to_all x1, blocking collectives, per_device(): lax.all_to_all(mine.reshape(length, groups * portion), 'ctx', split_axis=...  23.4 us
    pallas_call x1, Pallas kernels, per_device(): call(forward_kernel, [(length, triple) + tile, (length,) + tile, (length,...  17.1 us
    dot_general x1, matrix products, per_device(): lax.dot_general(cotangent, out_weight, (((1,), (1,)), ((), ())), preferre...  12.2 us
    all_gather x1, waiting for transfers between devices, per_device(): block_cotangent = lax.all_gather(swapped, 'tp', axis=1, tiled=True)  8.23 us
    unnamed x22, local copies, waits for them, and re-layouts  6.88 us
    dot_general x1, matrix products, per_device(): lax.dot_general(block_cotangent, gated_all, (((0,), (0,)), ((), ())), pre...  6.62 us
    all_to_all x2, local copies, waits for them, and re-layouts, per_device(): lax.all_to_all(mine.reshape(length, groups * portion), 'ctx', split_axis=...  3.93 us
  transfers between devices with their start and end apart: 4, of which 1 were waited for; matrix products, arithmetic and copies ran while one was open for 17% of the time, Pallas kernels for 40%

profile of v2, /device:TPU:13, one launch (start us, length us, event | category | flops | bytes accessed | tf_op | source)
XLA Modules:
  0.0 138.9 jit_solution(11117162326920476774)
XLA Ops:
  7.2 0.0 copy-start.3
  7.2 0.0 copy-start.6
  7.2 0.0 all-gather.4.cloned.1.call-start
  7.2 2.1 %copy.31 = bf16[128,2048]{0,1:T(8,128)(2,1)} copy(bf16[128,2048]{1,0:T(8,128)(2,1)} %param.11) | data formatting | bytes 1048576 | tf_op args[5]
  9.4 0.0 all-gather.4.cloned.1.call-update
  9.4 0.0 all-gather.8.cloned.1.call-start
  9.4 0.8 slice.12
  10.2 3.1 %collective-permute-start = (bf16[2,3,1024]{2,0,1:T(2,128)(2,1)S(1)}, bf16[2,3,1024]{2,0,1:T(2,128)(2,1)S(1)}, u32[]{:S(2)}, u32[]{:S(2)}) collective-permute-start(bf16[2,3,1024]{2,0,1:T(2,128)(2,1)S(1)} %slice.12), channel_id=1, source_target_pairs={{0,4},{4,8},{8,12},{12,16},{16,20},{20,24},{24,28},{1,5},{5,9},{9,... | collective-permute-start | bytes 36872 | tf_op jit(solution)/shard_map/ppermute | solution.py:16
  13.4 0.9 copy.39
  14.3 0.9 exponential_bitcast_fusion
  15.2 0.0 copy-start.4
  15.2 0.6 copy-done.4
  15.9 0.0 copy-done.3
  15.9 0.4 copy.28
  16.3 0.0 copy-done.6
  16.3 0.5 copy.30
  16.7 0.0 collective-permute-done
  16.8 0.1 maximum_convert_fusion.padded_ref
  16.9 0.0 copy-start
  16.9 17.1 %shard_map.101 = (f32[128,3,8,128]{3,2,1,0:T(8,128)S(1)}, f32[128,8,128]{2,1,0:T(8,128)S(1)}, f32[128,8,128]{2,1,0:T(8,128)S(1)}, f32[16,8,128]{2,1,0:T(8,128)S(1)}) custom-call(f32[130,3,8,128]{3,2,1,0:T(8,128)S(1)} %maximum_convert_fusion.padded_ref, f32[3,3,8,128]{3,2,1,0:T(8,128)S(1)} %reshape.52.taps_ref, ...), custom_call_target="tpu_custom_call" | custom-call | tf_op jit(solution)/shard_map/pallas_call | solution.py:300
  34.0 0.0 copy-start.1
  34.0 0.8 copy-done.1
  34.8 0.8 copy.50
  35.6 0.0 all-gather.8.cloned.1.call-update
  35.6 0.0 all-gather.6.cloned.1.call-start
  35.7 0.0 all-gather.4.cloned.1.call-done
  35.7 1.9 %dynamic-slice_bitcast_fusion = bf16[128,8,256]{0,2,1:T(8,128)(2,1)} fusion(bf16[128,8,4,256]{0,3,2,1:T(8,128)(2,1)} %bitcast.49, s32[]{:T(128)S(6)} %select_n.4), kind=kLoop, calls=%fused_computation.2 | loop fusion | bytes 1048580 | tf_op jit(solution)/shard_map/all_to_all | solution.py:319
  37.6 0.0 copy-done
  37.6 2.1 %copy.34 = bf16[128,8,256]{2,0,1:T(8,128)(2,1)} copy(bf16[128,8,256]{0,2,1:T(8,128)(2,1)} %dynamic-slice_bitcast_fusion) | data formatting | bytes 1048576 | tf_op jit(solution)/shard_map/all_to_all | solution.py:319
  39.6 23.4 %all_to_all.19 = bf16[128,8,256]{2,0,1:T(8,128)(2,1)} all-to-all(bf16[128,8,256]{2,0,1:T(8,128)(2,1)} %copy.34), channel_id=1, replica_groups=mesh['ctx'=8,'tp'=4] {'ctx'}, dimensions={1} | all-to-all | bytes 1048576 | tf_op jit(solution)/shard_map/all_to_all | solution.py:319
  63.0 0.0 all-gather.6.cloned.1.call-update
  63.1 0.0 copy-start.2
  63.1 12.2 %convolution_bitcast_fusion = f32[16,8,8,128]{3,1,2,0:T(8,128)S(1)} fusion(bf16[128,8192]{0,1:T(8,128)(2,1)} %all-gather.4.cloned.1.call-done, bf16[1024,8192]{1,0:T(8,128)(2,1)} %param.10), kind=kOutput, calls=%fused_computation | convolution fusion | flops 2147483648 | bytes 19398656 | tf_op jit(solution)/shard_map/dot_general | solution.py:310
  75.2 0.1 copy.41
  75.3 0.0 copy-done.2
  75.4 39.0 %shard_map.102 = (f32[128,3,8,128]{3,2,1,0:T(8,128)S(1)}, f32[48,8,128]{2,1,0:T(8,128)S(1)}) custom-call(f32[130,3,8,128]{3,2,1,0:T(8,128)} %copy-done, f32[128,3,8,128]{3,2,1,0:T(8,128)S(1)} %get-tuple-element.11.short_ref, f32[128,8,128]{2,1,0:T(8,128)S(1)} %copy-done.2, f32[128,8,128]{2,1,0:T(8,128)S(1)} %bitcast.48, ...), custom_call_target="tpu_custom_call" | custom-call | tf_op jit(solution)/shard_map/pallas_call | solution.py:326
  114.3 0.1 convert_element_type.11
  114.5 0.0 copy-start.5
  114.5 0.5 copy.32
  115.0 1.2 copy.35
  116.2 0.6 reshape.58
  116.8 0.0 copy-done.5
  116.9 0.7 copy_bitcast_fusion.1
  117.6 0.0 all-gather.8.cloned.1.call-done
  117.6 8.2 %all-gather.6.cloned.1.call-done = bf16[1024,1024]{1,0:T(8,128)(2,1)} async-done(((bf16[1024,256]{1,0:T(8,128)(2,1)}), bf16[1024,1024]{1,0:T(8,128)(2,1)}) %all-gather.6.cloned.1.call-update) | async-done | bytes 2097168 | tf_op jit(solution)/shard_map/all_gather | solution.py:322
  125.8 6.6 %fusion.2 = f32[1024,1024]{1,0:T(8,128)} fusion(bf16[1024,1024]{1,0:T(8,128)(2,1)} %all-gather.6.cloned.1.call-done, bf16[1024,1024]{1,0:T(8,128)(2,1)} %all-gather.8.cloned.1.call-done), kind=kOutput, calls=%fused_computation.15 | convolution fusion | flops 2147483648 | bytes 8388608 | tf_op jit(solution)/shard_map/dot_general | solution.py:338
  (9 shorter events, 0.2 us)
Async XLA Ops:
  7.2 8.7 %copy-start.3 = (bf16[128,3,1024]{2,0,1:T(8,128)(2,1)S(1)}, bf16[128,3,1024]{2,0,1:T(8,128)(2,1)}, u32[]{:S(2)}) copy-start(bf16[128,3,1024]{2,0,1:T(8,128)(2,1)} %param.6) | copy-start | bytes 2359300
  7.2 9.1 %copy-start.6 = (f32[3,3,1024]{2,1,0:T(4,128)S(1)}, f32[3,3,1024]{2,1,0:T(4,128)}, u32[]{:S(2)}) copy-start(f32[3,3,1024]{2,1,0:T(4,128)} %param.7) | copy-start | bytes 110596
  7.2 28.5 %all-gather.4.cloned.1.call-start = ((), (), s32[]{:S(2)}) async-start(), calls=%async_computation.1 | async-start | bytes 2621440 | tf_op jit(solution)/shard_map/all_gather | solution.py:289
  9.4 108.2 %all-gather.8.cloned.1.call-start = ((), (), s32[]{:S(2)}) async-start(), calls=%async_computation.3 | async-start | bytes 2359296 | tf_op jit(solution)/shard_map/all_gather | solution.py:306
  10.2 6.5 %collective-permute-start = (bf16[2,3,1024]{2,0,1:T(2,128)(2,1)S(1)}, bf16[2,3,1024]{2,0,1:T(2,128)(2,1)S(1)}, u32[]{:S(2)}, u32[]{:S(2)}) collective-permute-start(bf16[2,3,1024]{2,0,1:T(2,128)(2,1)S(1)} %slice.12), channel_id=1, source_target_pairs={{0,4},{4,8},{8,12},{12,16},{16,20},{20,24},{24,28},{1,5},{5,9},{9,... | collective-permute-start | bytes 36872 | tf_op jit(solution)/shard_map/ppermute | solution.py:16
  15.2 0.6 copy-start.4
  16.9 20.7 %copy-start = (f32[130,3,8,128]{3,2,1,0:T(8,128)}, f32[130,3,8,128]{3,2,1,0:T(8,128)S(1)}, u32[]{:S(2)}) copy-start(f32[130,3,8,128]{3,2,1,0:T(8,128)S(1)} %maximum_convert_fusion.padded_ref) | copy-start | bytes 4792324
  34.0 0.8 copy-start.1
  35.6 90.2 %all-gather.6.cloned.1.call-start = ((), (), s32[]{:S(2)}) async-start(), calls=%async_computation.2 | async-start | bytes 2621440 | tf_op jit(solution)/shard_map/all_gather | solution.py:322
  63.1 12.3 %copy-start.2 = (f32[128,8,128]{2,1,0:T(8,128)S(1)}, f32[128,8,128]{2,1,0:T(8,128)}, u32[]{:S(2)}) copy-start(f32[128,8,128]{2,1,0:T(8,128)} %copy-done.1) | copy-start | bytes 1572868
  114.5 2.4 %copy-start.5 = (f32[2,8,8,128]{3,2,1,0:T(8,128)S(1)}, f32[2,8,8,128]{3,2,1,0:T(8,128)}, u32[]{:S(2)}) copy-start(f32[2,8,8,128]{3,2,1,0:T(8,128)} %copy-done.4) | copy-start | bytes 196612
Sparse Core Ops, SparseCore 0:
  9.6 24.0 all-gather.3
  35.8 61.8 all-gather.7
  99.3 26.4 all-gather.5

commit v3 on v2

--- a/solution.py
+++ b/solution.py
@@ -10,44 +10,90 @@
 LANES = 128
 
 
-def shifted(value, axis, steps):
-    count = lax.axis_size(axis)
-    first, last = (max(0, -steps), min(count, count - steps))
-    return lax.ppermute(value, axis, [(source, source + steps) for source in range(first, last)])
-
-
 def rounded(value):
     return value.astype(BF16).astype(F32)
 
 
-def peer(offset):
-    count = lax.axis_size("ctx")
-    return lax.rem(lax.axis_index("ctx") + offset + count, count)
-
-
-def greet():
+def peer(offset, axis="ctx"):
+    count = lax.axis_size(axis)
+    return lax.rem(lax.axis_index(axis) + offset + count, count)
+
+
+def greet(axes):
     barrier = pltpu.get_barrier_semaphore()
-    for offset in range(1, lax.axis_size("ctx")):
-        pl.semaphore_signal(
-            barrier, inc=1, device_id={"ctx": peer(offset)}, device_id_type=pl.DeviceIdType.MESH
-        )
-
-
-def await_greetings():
-    pl.semaphore_wait(pltpu.get_barrier_semaphore(), lax.axis_size("ctx") - 1)
-
-
-def push(source, target, send_sem, recv_sem, offset):
-    copy = pltpu.make_async_remote_copy(
+    for axis in axes:
+        for offset in range(1, lax.axis_size(axis)):
+            pl.semaphore_signal(
+                barrier,
+                inc=1,
+                device_id={axis: peer(offset, axis)},
+                device_id_type=pl.DeviceIdType.MESH,
+            )
+
+
+def await_greetings(axes):
+    pl.semaphore_wait(
+        pltpu.get_barrier_semaphore(), sum(lax.axis_size(axis) - 1 for axis in axes)
+    )
+
+
+def remote(source, target, send_sem, recv_sem, offset, axis="ctx"):
+    return pltpu.make_async_remote_copy(
         src_ref=source,
         dst_ref=target,
         send_sem=send_sem,
         recv_sem=recv_sem,
-        device_id={"ctx": peer(offset)},
+        device_id={axis: peer(offset, axis)},
         device_id_type=pl.DeviceIdType.MESH,
     )
+
+
+def push(*arguments):
+    copy = remote(*arguments)
     copy.start()
     return copy
+
+
+def send_states(own, arrived, send_sems, recv_sems, direction):
+    count = lax.axis_size("ctx")
+    position = lax.axis_index("ctx")
+    sends = []
+    for k in range(1, count):
+        copy = remote(own, arrived.at[position], send_sems.at[k], recv_sems.at[k], direction * k)
+        if direction > 0:
+            has_target, has_source = position + k < count, position >= k
+        else:
+            has_target, has_source = position >= k, position + k < count
+
+        @pl.when(has_target)
+        def start():
+            copy.start()
+
+        sends.append((copy, has_target, has_source))
+    return sends
+
+
+def await_states(sends):
+    for copy, has_target, has_source in sends:
+
+        @pl.when(has_source)
+        def received():
+            copy.wait_recv()
+
+        @pl.when(has_target)
+        def sent():
+            copy.wait_send()
+
+
+def carry_states(state, arrived, block_decay, direction):
+    count = lax.axis_size("ctx")
+    position = lax.axis_index("ctx")
+    state[...] = jnp.zeros(state.shape, F32)
+    for block in range(count - 1) if direction > 0 else range(count - 1, 0, -1):
+
+        @pl.when(block < position if direction > 0 else block > position)
+        def add():
+            state[...] = block_decay[...] * state[...] + arrived[block]
 
 
 def tree_sum(terms):
@@ -58,26 +104,45 @@
 
 
 def forward_kernel(
-    padded_ref, taps_ref, decay_ref, block_decay_ref, amp_ref,
-    short_ref, gated_ref, convolved_ref, past_ref,
-    own, arrived, send_sems, recv_sems,
+    features_ref, taps_ref, decay_ref, block_decay_ref, amp_ref,
+    short_ref, gated_ref, convolved_ref, past_ref, padded_ref,
+    own, arrived, send_sems, recv_sems, rim_send, rim_recv,
 ):
     modes = decay_ref.shape[0]
     length = short_ref.shape[0]
     tap_count = taps_ref.shape[0]
-    count = lax.axis_size("ctx")
-    position = lax.axis_index("ctx")
-    greet()
+    rim = tap_count - 1
+    greet(("ctx",))
+
+    def copy_step(t, carry):
+        for j in range(3):
+            padded_ref[t + rim, j] = features_ref[t, j]
+        return carry
+
+    lax.fori_loop(0, length, copy_step, 0, unroll=4)
+    await_greetings(("ctx",))
+    rim_copy = push(
+        features_ref.at[pl.ds(length - rim, rim)], padded_ref.at[pl.ds(0, rim)],
+        rim_send.at[0], rim_recv.at[0], 1,
+    )
 
     def filter_step(t, carry):
         for j in range(3):
-            total = taps_ref[0, j] * padded_ref[t + tap_count - 1, j]
+            total = taps_ref[0, j] * padded_ref[t + rim, j]
             for lag in range(1, tap_count):
-                total = total + taps_ref[lag, j] * padded_ref[t + tap_count - 1 - lag, j]
+                total = total + taps_ref[lag, j] * padded_ref[t + rim - lag, j]
             short_ref[t, j] = total
         return carry
 
-    lax.fori_loop(0, length, filter_step, 0, unroll=4)
+    lax.fori_loop(rim, length, filter_step, 0, unroll=2)
+    rim_copy.wait()
+
+    @pl.when(lax.axis_index("ctx") == 0)
+    def clear():
+        padded_ref[pl.ds(0, rim)] = jnp.zeros((rim,) + padded_ref.shape[1:], F32)
+
+    for t in range(rim):
+        filter_step(t, 0)
     decays = [decay_ref[r] for r in range(modes)]
     zero = jnp.zeros(decay_ref.shape[1:], F32)
 
@@ -89,19 +154,8 @@
     for r in range(modes):
         own[r] = final[r]
 
-    await_greetings()
-    copies = [
-        push(own, arrived.at[position], send_sems.at[k], recv_sems.at[k], k)
-        for k in range(1, count)
-    ]
-    arrived[position] = own[...]
-    for copy in copies:
-        copy.wait()
-    past_ref[...] = jnp.zeros(past_ref.shape, F32)
-    for block in range(count - 1):
-        past_ref[...] = jnp.where(
-            block < position, block_decay_ref[...] * past_ref[...] + arrived[block], past_ref[...]
-        )
+    await_states(send_states(own, arrived, send_sems, recv_sems, 1))
+    carry_states(past_ref, arrived, block_decay_ref, 1)
 
     def step(t, states):
         product = rounded(short_ref[t, 1] * short_ref[t, 2])
@@ -116,10 +170,11 @@
 
 def backward_kernel(
     padded_ref, short_ref, convolved_ref, grad_gated_ref, taps_ref, decay_ref, block_decay_ref,
-    amp_ref, past_ref,
-    grad_features_ref, total_ref,
+    amp_ref, past_ref, mine_ref,
+    grad_features_ref, total_ref, block_ref,
     own, arrived, future, history, grad_conv, grad_short, readout, tail, packed, pieces, summed,
     state_send, state_recv, piece_send, piece_recv, sum_send, sum_recv, tail_send, tail_recv,
+    swap_send, swap_recv, spread_send, spread_recv,
 ):
     modes = decay_ref.shape[0]
     length = short_ref.shape[0]
@@ -129,7 +184,9 @@
     position = lax.axis_index("ctx")
     zero = jnp.zeros(decay_ref.shape[1:], F32)
     decays = [decay_ref[r] for r in range(modes)]
-    greet()
+    ranks = lax.axis_size("tp")
+    rank = lax.axis_index("tp")
+    greet(("ctx", "tp"))
 
     def local_step(i, states):
         t = length - 1 - i
@@ -140,12 +197,15 @@
     final = lax.fori_loop(0, length, local_step, (zero,) * modes, unroll=4)
     for r in range(modes):
         own[r] = final[r]
-    await_greetings()
-    copies = [
-        push(own, arrived.at[position], state_send.at[k], state_recv.at[k], k)
+    await_greetings(("ctx", "tp"))
+    sends = send_states(own, arrived, state_send, state_recv, -1)
+    swaps = [
+        push(
+            mine_ref.at[peer(k)], block_ref.at[rank, position], swap_send.at[k], swap_recv.at[k], k
+        )
         for k in range(1, count)
     ]
-    arrived[position] = own[...]
+    block_ref[rank, position] = mine_ref[position]
 
     for r in range(modes):
         history[0, r] = past_ref[r]
@@ -160,13 +220,8 @@
 
     lax.fori_loop(0, length, forward, tuple(past_ref[r] for r in range(modes)), unroll=2)
 
-    for copy in copies:
-        copy.wait()
-    future[...] = jnp.zeros(future.shape, F32)
-    for block in range(count - 1, 0, -1):
-        future[...] = jnp.where(
-            block > position, block_decay_ref[...] * future[...] + arrived[block], future[...]
-        )
+    await_states(sends)
+    carry_states(future, arrived, block_decay_ref, -1)
 
     half = modes // 2
     base = 3 * tap_count
@@ -189,6 +244,17 @@
                 grad_short[t, 2] = grad_product * short_ref[t, 1]
             return new, grad_amp, grad_decay
 
+        if group == 1:
+            for copy in swaps:
+                copy.wait()
+            spreads = [
+                push(
+                    block_ref.at[rank], block_ref.at[rank],
+                    spread_send.at[k], spread_recv.at[k], k, "tp",
+                )
+                for k in range(1, ranks)
+            ]
+
         start = (tuple(future[r] for r in picks), (zero,) * half, (zero,) * half)
         unused, grad_amp, grad_decay = lax.fori_loop(0, length, backward, start, unroll=2)
         for k, r in enumerate(picks):
@@ -257,14 +323,17 @@
                     later = jnp.where(inner, tail[t + lag - length, j], 0.0)
                 total = total + taps_ref[lag, j] * later
             grad_features_ref[t, j] = total
-    for copy in copies:
+    for copy in copies + spreads:
         copy.wait()
 
 
 def call(kernel, outs, scratch, identity, mib=48):
     return pl.pallas_call(
         kernel,
-        out_shape=[jax.ShapeDtypeStruct(shape, F32) for shape in outs],
+        out_shape=[
+            item if isinstance(item, jax.ShapeDtypeStruct) else jax.ShapeDtypeStruct(item, F32)
+            for item in outs
+        ],
         scratch_shapes=[
             pltpu.SemaphoreType.DMA((item,)) if isinstance(item, int) else pltpu.VMEM(item, F32)
             for item in scratch
@@ -287,9 +356,7 @@
     state = (modes,) + tile
 
     cotangent = lax.all_gather(grad_out, "tp", axis=1, tiled=True)
-    rim_rows = shifted(features[length - (tap_count - 1) :], "ctx", 1)
-    padded = jnp.concatenate([rim_rows, features], axis=0).astype(F32)
-    padded = padded.reshape((length + tap_count - 1, triple) + tile)
+    values = features.astype(F32).reshape((length, triple) + tile)
     taps = short_taps.reshape((tap_count, triple) + tile)
     half_rate = jnp.exp(0.5 * log_rate).reshape(state)
     rate = jnp.exp(log_rate).reshape(state)
@@ -297,12 +364,15 @@
     decay = jnp.exp(-rate)
     block_decay = jnp.exp(-rate * length)
 
-    short, gated, convolved, past = call(
+    short, gated, convolved, past, padded = call(
         forward_kernel,
-        [(length, triple) + tile, (length,) + tile, (length,) + tile, state],
-        [state, (groups,) + state, groups, groups],
+        [
+            (length, triple) + tile, (length,) + tile, (length,) + tile, state,
+            (length + tap_count - 1, triple) + tile,
+        ],
+        [state, (groups,) + state, groups, groups, 1, 1],
         0,
-    )(padded, taps, decay, block_decay, amp)
+    )(values, taps, decay, block_decay, amp)
     gated_all = lax.all_gather(
         gated.astype(BF16).reshape(length, width), "ctx", axis=0, tiled=True
     )
@@ -313,31 +383,37 @@
 
     features_out = cotangent.shape[1]
     portion = features_out // (groups * ranks)
-    mine = lax.dynamic_index_in_dim(
-        cotangent.reshape(length, groups, ranks, portion), rank, 2, keepdims=False
-    )
-    swapped = lax.all_to_all(
-        mine.reshape(length, groups * portion), "ctx", split_axis=1, concat_axis=0, tiled=True
-    )
-    block_cotangent = lax.all_gather(swapped, "tp", axis=1, tiled=True)
+    mine = jnp.stack(
+        [
+            lax.dynamic_slice_in_dim(cotangent, (group * ranks + rank) * portion, portion, 1)
+            for group in range(groups)
+        ]
+    )
 
     base = tap_count * triple
     share = -(-(base + 2 * modes) // groups)
-    grad_features, total = call(
+    grad_features, total, block_cotangent = call(
         backward_kernel,
-        [(length, triple) + tile, (groups * share,) + tile],
+        [
+            (length, triple) + tile,
+            (groups * share,) + tile,
+            jax.ShapeDtypeStruct((ranks, groups, length, portion), BF16),
+        ],
         [
             state, (groups,) + state, state, (length + 1,) + state, (length,) + tile,
             (length, triple) + tile, (length,) + tile, (tap_count - 1, triple) + tile,
             (groups * share,) + tile, (groups, share) + tile, (share,) + tile,
-            groups, groups, groups, groups, groups, groups, 1, 1,
+            groups, groups, groups, groups, groups, groups, 1, 1, groups, groups, ranks, ranks,
         ],
         1,
-    )(padded, short, convolved, grad_gated, taps, decay, block_decay, amp, past)
+    )(padded, short, convolved, grad_gated, taps, decay, block_decay, amp, past, mine)
 
     grad_weight_t = lax.dot_general(
-        block_cotangent, gated_all, (((0,), (0,)), ((), ())), preferred_element_type=F32
-    )
+        block_cotangent.reshape(ranks, groups * length, portion),
+        gated_all,
+        (((1,), (0,)), ((), ())),
+        preferred_element_type=F32,
+    ).reshape(ranks * portion, width)
     grad_taps = total[:base].reshape(tap_count, triple, width)
     grad_amp = total[base : base + modes]
     grad_decay = total[base + modes : base + 2 * modes]

time: 141 us -> 144 us (1.021)
  Pallas kernels: 56.1 us -> 82 us
  blocking collectives: 23.4 us -> 0 us
  local copies, waits for them, and re-layouts: 14 us -> 20.8 us
  starting transfers between devices: 3.27 us -> 0.08 us
  waiting for transfers between devices: 8.3 us -> 6.03 us
    pallas_call x1, Pallas kernels: 39 us -> 68.9 us  [per_device(): call(backward_kernel, [(length, triple) + tile, (groups * share,) + tile,...]
    all_to_all x1 -> x0, blocking collectives: 23.4 us -> none  [per_device(): lax.all_to_all(mine.reshape(length, groups * portion), 'ctx', split_axis=...]
    all_gather x1 -> x0, waiting for transfers between devices: 8.23 us -> none  [per_device(): block_cotangent = lax.all_gather(swapped, 'tp', axis=1, tiled=True)]
    unnamed x22 -> x26, local copies, waits for them, and re-layouts: 6.88 us -> 13.6 us
    all_gather x1, waiting for transfers between devices: 0.02 us -> 5.34 us  [per_device(): cotangent = lax.all_gather(grad_out, 'tp', axis=1, tiled=True)]
    pallas_call x1, Pallas kernels: 17.1 us -> 13 us  [per_device(): call(forward_kernel, [(length, triple) + tile, (length,) + tile, (length,...]
    all_to_all x2 -> x0, local copies, waits for them, and re-layouts: 3.93 us -> none  [per_device(): lax.all_to_all(mine.reshape(length, groups * portion), 'ctx', split_axis=...]
    reshape x1 -> x2, local copies, waits for them, and re-layouts: 0.68 us -> 4.39 us  [the longest x1 3.95 us: per_device(): block_cotangent.reshape(ranks, groups * length, portion)]
  transfers between devices with their start and end apart: 4 -> 2, of which waited for: 1 -> 1; matrix products, arithmetic and copies ran while one was open for 17% -> 22% of each run, Pallas kernels for 40% -> 57%
where the time goes in v3:
time: 144 us; the launch traced here: 143 us
  Pallas kernels  82 us (57%)
  local copies, waits for them, and re-layouts  20.8 us (14%)
  matrix products  18.6 us (13%)
  between operations  14.2 us (10%)
  waiting for transfers between devices  6.03 us (4%)
    pallas_call x1, Pallas kernels, per_device(): call(backward_kernel, [(length, triple) + tile, (groups * share,) + tile,...  68.9 us
    unnamed x26, local copies, waits for them, and re-layouts  13.6 us
    pallas_call x1, Pallas kernels, per_device(): call(forward_kernel, [(length, triple) + tile, (length,) + tile, (length,...  13 us
    dot_general x1, matrix products, per_device(): lax.dot_general(cotangent, out_weight, (((1,), (1,)), ((), ())), preferre...  12.1 us
    dot_general x1, matrix products, per_device(): lax.dot_general(block_cotangent.reshape(ranks, groups * length, portion),...  6.57 us
    all_gather x1, waiting for transfers between devices, per_device(): cotangent = lax.all_gather(grad_out, 'tp', axis=1, tiled=True)  5.34 us
    reshape x1, local copies, waits for them, and re-layouts, per_device(): block_cotangent.reshape(ranks, groups * length, portion)  3.95 us
  transfers between devices with their start and end apart: 2, of which 1 were waited for; matrix products, arithmetic and copies ran while one was open for 22% of the time, Pallas kernels for 57%

profile of v3, /device:TPU:13, one launch (start us, length us, event | category | flops | bytes accessed | tf_op | source)
XLA Modules:
  0.0 142.8 jit_solution(5475264184008771346)
XLA Ops:
  7.2 0.0 all-gather.3.cloned.1.call-start
  7.2 0.7 all-gather.3.cloned.1.call-update
  7.9 0.0 all-gather.5.cloned.1.call-start
  7.9 0.8 reshape.52.taps_ref
  8.8 0.9 copy.19
  9.6 0.9 exponential_bitcast_fusion
  10.5 0.0 copy-start.3
  10.6 1.5 %copy.13 = bf16[128,3,1024]{0,2,1:T(8,128)(2,1)S(1)} copy(bf16[128,3,1024]{2,0,1:T(8,128)(2,1)} %param.6) | data formatting | bytes 1572864 | tf_op args[0]
  12.1 0.4 copy.14.features_ref
  12.6 0.0 copy-done.3
  12.6 13.0 %shard_map.101 = (f32[128,3,8,128]{3,2,1,0:T(8,128)S(1)}, f32[128,8,128]{2,1,0:T(8,128)S(1)}, f32[128,8,128]{2,1,0:T(8,128)S(1)}, f32[16,8,128]{2,1,0:T(8,128)S(1)}, f32[130,3,8,128]{3,2,1,0:T(8,128)S(1)}) custom-call(f32[128,3,8,128]{3,2,1,0:T(8,128)S(1)} %copy.14.features_ref, f32[3,3,8,128]{3,2,1,0:T(8,128)S(1)} %reshape.52.taps_ref, ...), custom_call_target="tpu_custom_call" | custom-call | tf_op jit(solution)/shard_map/pallas_call | solution.py:367
  25.6 0.0 copy-start
  25.6 1.1 copy-done
  26.8 0.0 copy-start.1
  26.8 0.8 copy-done.1
  27.6 0.8 copy.28
  28.3 0.0 all-gather.5.cloned.1.call-update
  28.4 5.3 %all-gather.3.cloned.1.call-done = bf16[128,8192]{1,0:T(8,128)(2,1)} async-done(((bf16[128,2048]{1,0:T(8,128)(2,1)}), bf16[128,8192]{1,0:T(8,128)(2,1)}) %all-gather.3.cloned.1.call-update) | async-done | bytes 2097168 | tf_op jit(solution)/shard_map/all_gather | solution.py:358
  33.7 12.1 %convolution_bitcast_fusion = f32[16,8,8,128]{3,1,2,0:T(8,128)S(1)} fusion(bf16[128,8192]{1,0:T(8,128)(2,1)} %all-gather.3.cloned.1.call-done, bf16[1024,8192]{1,0:T(8,128)(2,1)} %param.10), kind=kOutput, calls=%fused_computation | convolution fusion | flops 2147483648 | bytes 19398656 | tf_op jit(solution)/shard_map/dot_general | solution.py:380
  45.8 0.0 copy-start.2
  45.8 0.1 copy.21
  45.9 0.9 bitcast_dynamic-update-slice_fusion.7
  46.8 0.8 bitcast_dynamic-update-slice_fusion.6
  47.6 0.8 bitcast_dynamic-update-slice_fusion.5
  48.5 0.8 bitcast_dynamic-update-slice_fusion.4
  49.3 0.8 bitcast_dynamic-update-slice_fusion.3
  50.2 0.8 bitcast_dynamic-update-slice_fusion.2
  51.0 0.8 bitcast_dynamic-update-slice_fusion.1
  51.9 0.8 bitcast_dynamic-update-slice_fusion.mine_ref
  52.7 0.0 copy-done.2
  52.7 0.0 copy-start.4
  52.7 68.9 %shard_map.102 = (f32[128,3,8,128]{3,2,1,0:T(8,128)S(1)}, f32[48,8,128]{2,1,0:T(8,128)S(1)}, bf16[4,8,128,256]{3,2,1,0:T(8,128)(2,1)}) custom-call(f32[130,3,8,128]{3,2,1,0:T(8,128)} %copy-done, f32[128,3,8,128]{3,2,1,0:T(8,128)S(1)} %get-tuple-element.14.short_ref, f32[128,8,128]{2,1,0:T(8,128)S(1)} %copy-done.2, f32[128,8,128]{2,1,0:T(8,128)S(1)} %bitcast.63, ...), custom_call_target="tpu_custom_call" | custom-call | tf_op jit(solution)/shard_map/pallas_call | solution.py:395
  121.7 0.0 copy-done.4
  121.7 0.6 copy.29
  122.4 0.6 copy.30
  123.0 0.1 convert_element_type.7
  123.1 0.5 copy.15
  123.7 1.2 copy.17
  124.8 4.0 %copy.16 = bf16[4,1024,256]{1,2,0:T(8,128)(2,1)} copy(bf16[4,1024,256]{2,1,0:T(8,128)(2,1)} %bitcast.66) | data formatting | bytes 4194304 | tf_op jit(solution)/shard_map/reshape | solution.py:412
  128.8 0.6 reshape.58
  129.4 0.0 all-gather.5.cloned.1.call-done
  129.4 6.6 %fusion.2 = f32[1024,1024]{1,0:T(8,128)} fusion(bf16[1024,1024]{1,0:T(8,128)(2,1)} %bitcast.67, bf16[1024,1024]{1,0:T(8,128)(2,1)} %all-gather.5.cloned.1.call-done), kind=kOutput, calls=%fused_computation.21 | convolution fusion | flops 2147483648 | bytes 8388608 | tf_op jit(solution)/shard_map/dot_general | solution.py:411
  (6 shorter events, 0.1 us)
Async XLA Ops:
  7.2 26.5 %all-gather.3.cloned.1.call-start = ((), (), s32[]{:S(2)}) async-start(), calls=%async_computation | async-start | bytes 2621440 | tf_op jit(solution)/shard_map/all_gather | solution.py:358
  7.9 121.5 %all-gather.5.cloned.1.call-start = ((), (), s32[]{:S(2)}) async-start(), calls=%async_computation.1 | async-start | bytes 2359296 | tf_op jit(solution)/shard_map/all_gather | solution.py:376
  10.5 2.0 %copy-start.3 = (f32[2,8,8,128]{3,2,1,0:T(8,128)}, f32[2,8,8,128]{3,2,1,0:T(8,128)S(1)}, u32[]{:S(2)}) copy-start(f32[2,8,8,128]{3,2,1,0:T(8,128)S(1)} %copy.18) | copy-start | bytes 196612
  25.6 1.2 copy-start
  26.8 0.8 copy-start.1
  45.8 6.9 %copy-start.2 = (f32[128,8,128]{2,1,0:T(8,128)S(1)}, f32[128,8,128]{2,1,0:T(8,128)}, u32[]{:S(2)}) copy-start(f32[128,8,128]{2,1,0:T(8,128)} %copy-done.1) | copy-start | bytes 1572868
  52.7 69.0 %copy-start.4 = (f32[2,8,8,128]{3,2,1,0:T(8,128)S(1)}, f32[2,8,8,128]{3,2,1,0:T(8,128)}, u32[]{:S(2)}) copy-start(f32[2,8,8,128]{3,2,1,0:T(8,128)} %copy-done.3) | copy-start | bytes 196612
Sparse Core Ops, SparseCore 0:
  9.6 24.0 all-gather.2
  35.8 64.4 all-gather.4

commit v4 on v3

--- a/solution.py
+++ b/solution.py
@@ -170,11 +170,10 @@
 
 def backward_kernel(
     padded_ref, short_ref, convolved_ref, grad_gated_ref, taps_ref, decay_ref, block_decay_ref,
-    amp_ref, past_ref, mine_ref,
-    grad_features_ref, total_ref, block_ref,
+    amp_ref, past_ref,
+    grad_features_ref, total_ref,
     own, arrived, future, history, grad_conv, grad_short, readout, tail, packed, pieces, summed,
     state_send, state_recv, piece_send, piece_recv, sum_send, sum_recv, tail_send, tail_recv,
-    swap_send, swap_recv, spread_send, spread_recv,
 ):
     modes = decay_ref.shape[0]
     length = short_ref.shape[0]
@@ -184,9 +183,7 @@
     position = lax.axis_index("ctx")
     zero = jnp.zeros(decay_ref.shape[1:], F32)
     decays = [decay_ref[r] for r in range(modes)]
-    ranks = lax.axis_size("tp")
-    rank = lax.axis_index("tp")
-    greet(("ctx", "tp"))
+    greet(("ctx",))
 
     def local_step(i, states):
         t = length - 1 - i
@@ -197,16 +194,8 @@
     final = lax.fori_loop(0, length, local_step, (zero,) * modes, unroll=4)
     for r in range(modes):
         own[r] = final[r]
-    await_greetings(("ctx", "tp"))
+    await_greetings(("ctx",))
     sends = send_states(own, arrived, state_send, state_recv, -1)
-    swaps = [
-        push(
-            mine_ref.at[peer(k)], block_ref.at[rank, position], swap_send.at[k], swap_recv.at[k], k
-        )
-        for k in range(1, count)
-    ]
-    block_ref[rank, position] = mine_ref[position]
-
     for r in range(modes):
         history[0, r] = past_ref[r]
 
@@ -244,17 +233,6 @@
                 grad_short[t, 2] = grad_product * short_ref[t, 1]
             return new, grad_amp, grad_decay
 
-        if group == 1:
-            for copy in swaps:
-                copy.wait()
-            spreads = [
-                push(
-                    block_ref.at[rank], block_ref.at[rank],
-                    spread_send.at[k], spread_recv.at[k], k, "tp",
-                )
-                for k in range(1, ranks)
-            ]
-
         start = (tuple(future[r] for r in picks), (zero,) * half, (zero,) * half)
         unused, grad_amp, grad_decay = lax.fori_loop(0, length, backward, start, unroll=2)
         for k, r in enumerate(picks):
@@ -323,7 +301,7 @@
                     later = jnp.where(inner, tail[t + lag - length, j], 0.0)
                 total = total + taps_ref[lag, j] * later
             grad_features_ref[t, j] = total
-    for copy in copies + spreads:
+    for copy in copies:
         copy.wait()
 
 
@@ -383,37 +361,34 @@
 
     features_out = cotangent.shape[1]
     portion = features_out // (groups * ranks)
-    mine = jnp.stack(
-        [
-            lax.dynamic_slice_in_dim(cotangent, (group * ranks + rank) * portion, portion, 1)
-            for group in range(groups)
-        ]
-    )
+    mine = lax.dynamic_index_in_dim(
+        cotangent.reshape(length, groups, ranks, portion), rank, 2, keepdims=False
+    )
+    swapped = lax.all_to_all(
+        mine.reshape(length, groups * portion), "ctx", split_axis=1, concat_axis=0, tiled=True
+    )
+    block_cotangent = lax.all_gather(swapped, "tp", axis=1, tiled=True)
 
     base = tap_count * triple
     share = -(-(base + 2 * modes) // groups)
-    grad_features, total, block_cotangent = call(
+    grad_features, total = call(
         backward_kernel,
         [
             (length, triple) + tile,
             (groups * share,) + tile,
-            jax.ShapeDtypeStruct((ranks, groups, length, portion), BF16),
         ],
         [
             state, (groups,) + state, state, (length + 1,) + state, (length,) + tile,
             (length, triple) + tile, (length,) + tile, (tap_count - 1, triple) + tile,
             (groups * share,) + tile, (groups, share) + tile, (share,) + tile,
-            groups, groups, groups, groups, groups, groups, 1, 1, groups, groups, ranks, ranks,
+            groups, groups, groups, groups, groups, groups, 1, 1,
         ],
         1,
-    )(padded, short, convolved, grad_gated, taps, decay, block_decay, amp, past, mine)
+    )(padded, short, convolved, grad_gated, taps, decay, block_decay, amp, past)
 
     grad_weight_t = lax.dot_general(
-        block_cotangent.reshape(ranks, groups * length, portion),
-        gated_all,
-        (((1,), (0,)), ((), ())),
-        preferred_element_type=F32,
-    ).reshape(ranks * portion, width)
+        block_cotangent, gated_all, (((0,), (0,)), ((), ())), preferred_element_type=F32
+    )
     grad_taps = total[:base].reshape(tap_count, triple, width)
     grad_amp = total[base : base + modes]
     grad_decay = total[base + modes : base + 2 * modes]

time: 144 us -> 139 us (0.965)
  Pallas kernels: 82 us -> 52.5 us
  blocking collectives: 0 us -> 23.9 us
  waiting for transfers between devices: 6.03 us -> 15.3 us
  local copies, waits for them, and re-layouts: 20.8 us -> 11.8 us
    pallas_call x1, Pallas kernels: 68.9 us -> 39.5 us  [per_device(): call(backward_kernel, [(length, triple) + tile, (groups * share,) + tile]...]
    all_to_all x0 -> x1, blocking collectives: none -> 23.9 us  [per_device(): lax.all_to_all(mine.reshape(length, groups * portion), 'ctx', split_axis=...]
    all_gather x0 -> x1, waiting for transfers between devices: none -> 10.4 us  [per_device(): block_cotangent = lax.all_gather(swapped, 'tp', axis=1, tiled=True)]
    unnamed x26 -> x20, local copies, waits for them, and re-layouts: 13.6 us -> 7.38 us
    reshape x1, local copies, waits for them, and re-layouts: 3.95 us -> 0.68 us  [per_device(): (0.5 * grad_amp * amp - grad_decay * amp * decay * rate).reshape(modes, w...]
  transfers between devices with their start and end apart: 2 -> 3, of which waited for: 1 -> 2; matrix products, arithmetic and copies ran while one was open for 22% -> 15% of each run, Pallas kernels for 57% -> 38%
where the time goes in v4:
time: 139 us; the launch traced here: 137 us
  Pallas kernels  52.5 us (38%)
  blocking collectives  23.9 us (17%)
  matrix products  18.8 us (14%)
  waiting for transfers between devices  15.3 us (11%)
  between operations  13.9 us (10%)
  local copies, waits for them, and re-layouts  11.8 us (8%)
    pallas_call x1, Pallas kernels, per_device(): call(backward_kernel, [(length, triple) + tile, (groups * share,) + tile]...  39.5 us
    all_to_all x1, blocking collectives, per_device(): lax.all_to_all(mine.reshape(length, groups * portion), 'ctx', split_axis=...  23.9 us
    pallas_call x1, Pallas kernels, per_device(): call(forward_kernel, [(length, triple) + tile, (length,) + tile, (length,...  13 us
    dot_general x1, matrix products, per_device(): lax.dot_general(cotangent, out_weight, (((1,), (1,)), ((), ())), preferre...  12.2 us
    all_gather x1, waiting for transfers between devices, per_device(): block_cotangent = lax.all_gather(swapped, 'tp', axis=1, tiled=True)  10.4 us
    unnamed x20, local copies, waits for them, and re-layouts  7.38 us
    dot_general x1, matrix products, per_device(): lax.dot_general(block_cotangent, gated_all, (((0,), (0,)), ((), ())), pre...  6.62 us
    all_gather x1, waiting for transfers between devices, per_device(): cotangent = lax.all_gather(grad_out, 'tp', axis=1, tiled=True)  4.92 us
  transfers between devices with their start and end apart: 3, of which 2 were waited for; matrix products, arithmetic and copies ran while one was open for 15% of the time, Pallas kernels for 38%

profile of v4, /device:TPU:13, one launch (start us, length us, event | category | flops | bytes accessed | tf_op | source)
XLA Modules:
  0.0 137.4 jit_solution(11143039718081546514)
XLA Ops:
  7.2 0.0 copy-start.3
  7.2 0.0 all-gather.4.cloned.1.call-start
  7.2 2.1 %copy.27 = bf16[128,2048]{0,1:T(8,128)(2,1)} copy(bf16[128,2048]{1,0:T(8,128)(2,1)} %param.11) | data formatting | bytes 1048576 | tf_op args[5]
  9.3 0.0 all-gather.4.cloned.1.call-update
  9.4 0.0 all-gather.8.cloned.1.call-start
  9.4 0.8 reshape.56.taps_ref
  10.2 0.9 copy.35
  11.1 0.9 exponential_bitcast_fusion
  12.0 0.0 copy-done.3
  12.0 0.0 copy-start.4
  12.0 0.4 copy.25
  12.4 0.4 copy.26.features_ref
  12.9 0.0 copy-done.4
  12.9 13.0 %shard_map.101 = (f32[128,3,8,128]{3,2,1,0:T(8,128)S(1)}, f32[128,8,128]{2,1,0:T(8,128)S(1)}, f32[128,8,128]{2,1,0:T(8,128)S(1)}, f32[16,8,128]{2,1,0:T(8,128)S(1)}, f32[130,3,8,128]{3,2,1,0:T(8,128)S(1)}) custom-call(f32[128,3,8,128]{3,2,1,0:T(8,128)S(1)} %copy.26.features_ref, f32[3,3,8,128]{3,2,1,0:T(8,128)S(1)} %reshape.56.taps_ref, ...), custom_call_target="tpu_custom_call" | custom-call | tf_op jit(solution)/shard_map/pallas_call | solution.py:345
  26.0 0.0 copy-start
  26.0 1.1 copy-done
  27.1 0.0 copy-start.1
  27.1 0.8 copy-done.1
  27.9 0.8 copy.44
  28.7 0.0 all-gather.8.cloned.1.call-update
  28.7 0.0 all-gather.6.cloned.1.call-start
  28.8 4.9 %all-gather.4.cloned.1.call-done = bf16[128,8192]{0,1:T(8,128)(2,1)} async-done(((bf16[128,2048]{0,1:T(8,128)(2,1)}), bf16[128,8192]{0,1:T(8,128)(2,1)}) %all-gather.4.cloned.1.call-update) | async-done | bytes 2097168 | tf_op jit(solution)/shard_map/all_gather | solution.py:336
  33.7 1.1 dynamic-slice_bitcast_fusion
  34.8 0.2 copy.30
  35.0 23.9 %all_to_all.19 = bf16[128,8,256]{2,0,1:T(8,128)(2,1)} all-to-all(bf16[128,8,256]{2,0,1:T(8,128)(2,1)S(1)} %copy.30), channel_id=1, replica_groups=mesh['ctx'=8,'tp'=4] {'ctx'}, dimensions={1} | all-to-all | bytes 1048576 | tf_op jit(solution)/shard_map/all_to_all | solution.py:367
  58.9 0.0 all-gather.6.cloned.1.call-update
  59.0 0.0 copy-start.2
  59.0 12.2 %convolution_bitcast_fusion = f32[16,8,8,128]{3,1,2,0:T(8,128)S(1)} fusion(bf16[128,8192]{0,1:T(8,128)(2,1)} %all-gather.4.cloned.1.call-done, bf16[1024,8192]{1,0:T(8,128)(2,1)} %param.10), kind=kOutput, calls=%fused_computation | convolution fusion | flops 2147483648 | bytes 19398656 | tf_op jit(solution)/shard_map/dot_general | solution.py:358
  71.2 0.1 copy.37
  71.3 0.0 copy-done.2
  71.3 39.5 %shard_map.102 = (f32[128,3,8,128]{3,2,1,0:T(8,128)S(1)}, f32[48,8,128]{2,1,0:T(8,128)S(1)}) custom-call(f32[130,3,8,128]{3,2,1,0:T(8,128)} %copy-done, f32[128,3,8,128]{3,2,1,0:T(8,128)S(1)} %get-tuple-element.13.short_ref, f32[128,8,128]{2,1,0:T(8,128)S(1)} %copy-done.2, f32[128,8,128]{2,1,0:T(8,128)S(1)} %bitcast.47, ...), custom_call_target="tpu_custom_call" | custom-call | tf_op jit(solution)/shard_map/pallas_call | solution.py:374
  110.7 0.1 convert_element_type.7
  110.8 0.0 copy-start.5
  110.9 0.5 copy.28
  111.4 1.2 copy.31
  112.6 0.6 reshape.62
  113.2 0.0 copy-done.5
  113.3 0.7 copy_bitcast_fusion.1
  113.9 0.0 all-gather.8.cloned.1.call-done
  113.9 10.4 %all-gather.6.cloned.1.call-done = bf16[1024,1024]{1,0:T(8,128)(2,1)} async-done(((bf16[1024,256]{1,0:T(8,128)(2,1)}), bf16[1024,1024]{1,0:T(8,128)(2,1)}) %all-gather.6.cloned.1.call-update) | async-done | bytes 2097168 | tf_op jit(solution)/shard_map/all_gather | solution.py:370
  124.3 6.6 %fusion.2 = f32[1024,1024]{1,0:T(8,128)} fusion(bf16[1024,1024]{1,0:T(8,128)(2,1)} %all-gather.6.cloned.1.call-done, bf16[1024,1024]{1,0:T(8,128)(2,1)} %all-gather.8.cloned.1.call-done), kind=kOutput, calls=%fused_computation.14 | convolution fusion | flops 2147483648 | bytes 8388608 | tf_op jit(solution)/shard_map/dot_general | solution.py:389
  (7 shorter events, 0.1 us)
Async XLA Ops:
  7.2 4.8 %copy-start.3 = (bf16[128,3,1024]{2,0,1:T(8,128)(2,1)S(1)}, bf16[128,3,1024]{2,0,1:T(8,128)(2,1)}, u32[]{:S(2)}) copy-start(bf16[128,3,1024]{2,0,1:T(8,128)(2,1)} %param.6) | copy-start | bytes 2359300
  7.2 26.5 %all-gather.4.cloned.1.call-start = ((), (), s32[]{:S(2)}) async-start(), calls=%async_computation.1 | async-start | bytes 2621440 | tf_op jit(solution)/shard_map/all_gather | solution.py:336
  9.4 104.6 %all-gather.8.cloned.1.call-start = ((), (), s32[]{:S(2)}) async-start(), calls=%async_computation.3 | async-start | bytes 2359296 | tf_op jit(solution)/shard_map/all_gather | solution.py:354
  12.0 0.9 copy-start.4
  26.0 1.2 copy-start
  27.1 0.8 copy-start.1
  28.7 95.6 %all-gather.6.cloned.1.call-start = ((), (), s32[]{:S(2)}) async-start(), calls=%async_computation.2 | async-start | bytes 2621440 | tf_op jit(solution)/shard_map/all_gather | solution.py:370
  59.0 12.3 %copy-start.2 = (f32[128,8,128]{2,1,0:T(8,128)S(1)}, f32[128,8,128]{2,1,0:T(8,128)}, u32[]{:S(2)}) copy-start(f32[128,8,128]{2,1,0:T(8,128)} %copy-done.1) | copy-start | bytes 1572868
  110.8 2.4 %copy-start.5 = (f32[2,8,8,128]{3,2,1,0:T(8,128)S(1)}, f32[2,8,8,128]{3,2,1,0:T(8,128)}, u32[]{:S(2)}) copy-start(f32[2,8,8,128]{3,2,1,0:T(8,128)} %copy-done.4) | copy-start | bytes 196612
Sparse Core Ops, SparseCore 0:
  9.6 24.0 all-gather.3
  35.8 60.4 all-gather.7
  97.9 26.3 all-gather.5
